TPU v7x, 256 devices: a whole 4x4x8 slice. The times are simulated.
256 devices in a mesh: section: 16 (over x_lo, y, core), tensor: 16 (over x_hi, z).
Axes of the slice: x: 4 (x_hi: 2, x_lo: 2; x = x_hi * 2 + x_lo), y: 4, z: 8, core: 2. Of those that a mesh axis runs over, the one named last changes fastest.
Arguments:
- queries: bfloat16 [1024, 128, 128], P('section', 'tensor'), may hold values from -48 to 48
- kv_pool: bfloat16 [8, 64, 128, 256], P(None, 'section'), may hold values from -16 to 16
- block_table: int32 [1024, 4], P('section'), may hold values from 0 to 3
- cached_lengths: int32 [1024], P('section'), may hold values from 2 to 512
- arrivals: bfloat16 [8, 128, 128, 256], P(None, 'section'), may hold values from -6 to 6
- arrival_section: int32 [128], P('section'), may hold values from 0 to 15, as said below
- arrival_row: int32 [128], P('section'), may hold values from 0 to 63
- out_weight: bfloat16 [16384, 12288], P('tensor', 'section'), may hold values from -0.046875 to 0.046875
- residual: bfloat16 [1024, 12288], P('tensor', 'section'), may hold values from -40 to 40
- norm_gain: bfloat16 [12288], P('section'), may hold values from 0.099609375 to 1.8984375
- gate_weight: bfloat16 [12288, 26624], P('section', 'tensor'), may hold values from -0.0546875 to 0.0546875
- up_weight: bfloat16 [12288, 26624], P('section', 'tensor'), may hold values from -0.0546875 to 0.0546875
Outputs:
- attn_proj: float32 [1024, 12288], P('tensor', 'section')
- hidden: float32 [1024, 26624], P('section', 'tensor')
Inputs may be any that keep to these rules, and one draw needn't show every extreme that they name: `arrival_section`: each section's 8 entries name one destination section at most 2 times; in every draw some destination section is named exactly 2 times by the entries of every section.
All inputs are finite; a program needn't handle non-finite values.
Results may differ from a plain program's by a relative error of at most 0.02.
Values may be sent and summed in bfloat16 or wider, within the bound.
A program may use at most 128 MiB of HBM per device.

v0:
```python
import jax
import jax.numpy as jnp
from jax import lax
from jax.sharding import PartitionSpec as P

CAP = 2


NEG_LARGE = -1e30
EPSILON = 1e-05


def cached_allowed(table_rows, lengths, slot_count, block_len):
    positions = jnp.arange(block_len)
    slot_ids = jnp.arange(slot_count)
    allowed = jnp.zeros((table_rows.shape[0], slot_count, block_len), dtype=bool)
    for column in range(table_rows.shape[1]):
        listed = table_rows[:, column][:, None] == slot_ids[None, :]
        inside = positions[None, :] < (lengths - column * block_len)[:, None]
        allowed = allowed | listed[:, :, None] & inside[:, None, :]
    return allowed.reshape(table_rows.shape[0], slot_count * block_len)


def partial_softmax(queries, tokens, allowed):
    head_dim = queries.shape[2]
    scores = jnp.einsum(
        "rhd,kd->rhk", queries, tokens[:, :head_dim], preferred_element_type=jnp.float32
    ) * head_dim ** (-0.5)
    token_mask = allowed[:, None, :]
    masked = jnp.where(token_mask, scores, NEG_LARGE)
    highest = jnp.max(masked, axis=2)
    weights = jnp.where(token_mask, jnp.exp(masked - highest[:, :, None]), 0.0)
    totals = jnp.sum(weights, axis=2)
    summed = jnp.einsum(
        "rhk,kd->rhd",
        weights.astype(jnp.bfloat16),
        tokens[:, head_dim:],
        preferred_element_type=jnp.float32,
    )
    return (highest, totals, summed)


def body(
    queries,
    kv_pool,
    block_table,
    cached_lengths,
    arrivals,
    arrival_section,
    arrival_row,
    out_weight,
    residual,
    norm_gain,
    gate_weight,
    up_weight,
):
    sections = lax.axis_size("section")
    tensor_id = lax.axis_index("tensor")
    kv_group = tensor_id // 2
    row_count = queries.shape[0]
    slot_count = kv_pool.shape[1]
    block_len = kv_pool.shape[2]
    features = kv_pool.shape[3]
    own_pool = lax.dynamic_index_in_dim(kv_pool, kv_group, 0, keepdims=False).reshape(
        slot_count * block_len, features
    )
    pool_allowed = cached_allowed(block_table, cached_lengths, slot_count, block_len)
    own_new = lax.dynamic_index_in_dim(arrivals, kv_group, 0, keepdims=False)
    sources = own_new.shape[0]
    entry_ids = jnp.arange(sources)
    same_dest = arrival_section[:, None] == arrival_section[None, :]
    earlier = same_dest & (entry_ids[None, :] < entry_ids[:, None])
    slot_rank = jnp.sum(earlier.astype(jnp.int32), axis=1)
    target = arrival_section * CAP + slot_rank
    placing = jnp.arange(sections * CAP)[:, None] == target[None, :]
    send_blocks = jnp.dot(
        placing.astype(jnp.bfloat16),
        own_new.reshape(sources, block_len * features),
        preferred_element_type=jnp.bfloat16,
    )
    send_blocks = send_blocks.reshape(sections, CAP, block_len, features)
    send_rows = (jnp.sum(jnp.where(placing, arrival_row[None, :] + 1, 0), axis=1) - 1).reshape(
        sections, CAP
    )
    got_blocks, got_rows = (
        lax.all_to_all(send_blocks, "section", split_axis=0, concat_axis=0, tiled=True),
        lax.all_to_all(send_rows, "section", split_axis=0, concat_axis=0, tiled=True),
    )
    arrived = got_blocks.reshape(sections * CAP * block_len, features)
    owner_match = got_rows.reshape(sections * CAP)[None, :] == jnp.arange(row_count)[:, None]
    new_allowed = jnp.broadcast_to(
        owner_match[:, :, None], (row_count, sections * CAP, block_len)
    ).reshape(row_count, sections * CAP * block_len)
    highest, totals, summed = partial_softmax(
        queries,
        jnp.concatenate([own_pool, arrived], 0),
        jnp.concatenate([pool_allowed, new_allowed], 1),
    )
    attention = (summed / totals[:, :, None]).astype(jnp.bfloat16).reshape(row_count, -1)
    partial_proj = jnp.dot(
        lax.all_gather(attention, "section", axis=0, tiled=True),
        out_weight,
        preferred_element_type=jnp.float32,
    )
    model_width = residual.shape[1] * sections
    attn_proj = lax.psum_scatter(partial_proj, "tensor", scatter_dimension=0, tiled=True)
    combined = residual.astype(jnp.float32) + attn_proj
    squares = lax.psum(jnp.sum(combined * combined, axis=1), "section")
    normed = (
        combined
        * norm_gain.astype(jnp.float32)[None, :]
        * lax.rsqrt(squares / model_width + EPSILON)[:, None]
    ).astype(jnp.bfloat16)
    segment = lax.all_gather(normed, "tensor", axis=0, tiled=True)
    gate_part = jnp.dot(segment, gate_weight, preferred_element_type=jnp.float32)
    up_part = jnp.dot(segment, up_weight, preferred_element_type=jnp.float32)
    both_terms = jnp.concatenate([gate_part, up_part], 1)
    gate_up = lax.psum_scatter(both_terms, "section", scatter_dimension=0, tiled=True)
    hidden_units = gate_weight.shape[1]
    hidden = jax.nn.silu(gate_up[:, :hidden_units]) * gate_up[:, hidden_units:]
    return (attn_proj, hidden)


def solution(mesh):
    placed = (
        P("section", "tensor", None),
        P(None, "section", None, None),
        P("section", None),
        P("section"),
        P(None, "section", None, None),
        P("section"),
        P("section"),
        P("tensor", "section"),
        P("tensor", "section"),
        P("section"),
        P("section", "tensor"),
        P("section", "tensor"),
    )
    return jax.shard_map(
        body,
        mesh=mesh,
        in_specs=placed,
        out_specs=(P("tensor", "section"), P("section", "tensor")),
        check_vma=False,
    )
```

profile of v0, /device:TPU:1, one launch (start us, length us, event | category | flops | bytes accessed | tf_op | source)
XLA Modules:
  0.0 531.8 jit_solution(796588167974416666)
XLA Ops:
  7.2 1.0 convert_reduce_fusion
  9.0 0.7 sub.34
  9.7 6.9 %all-to-all-start = ((s32[16,1,2]{2,1,0:T(1,128)}), s32[16,1,2]{2,1,0:T(1,128)S(1)}, u32[]{:S(2)}, u32[]{:S(2)}) async-start(s32[16,1,2]{2,1,0:T(1,128)} %bitcast.4), calls=%async_computation | async-start | bytes 16384 | tf_op jit(solution)/shard_map/all_to_all | solution.py:87
  17.3 1.1 dynamic-slice_bitcast_fusion
  18.3 0.8 fusion.35
  19.3 2.0 copy.27
  22.0 5.2 all-to-all-start.1
  27.9 1.0 constant_dynamic-slice_fusion
  30.7 24.6 %all-to-all-done.1 = bf16[16,2,128,256]{3,2,1,0:T(8,128)(2,1)} async-done(((bf16[16,2,128,256]{3,2,1,0:T(8,128)(2,1)}), bf16[16,2,128,256]{3,2,1,0:T(8,128)(2,1)}, u32[]{:S(2)}, u32[]{:S(2)}) %all-to-all-start.1) | async-done | bytes 2097184 | tf_op jit(solution)/shard_map/all_to_all | solution.py:86
  55.3 2.6 fusion.14
  57.9 4.3 fusion.2
  62.2 2.7 fusion.29
  65.8 40.2 %all-gather.3.cloned.1.call-done = bf16[1024,1024]{1,0:T(8,128)(2,1)} async-done(((bf16[64,1024]{1,0:T(8,128)(2,1)}), bf16[1024,1024]{1,0:T(8,128)(2,1)}) %all-gather.3.cloned.1.call-update) | async-done | bytes 2097168 | tf_op jit(solution)/shard_map/all_gather | solution.py:101
  106.0 5.5 %fusion.48 = f32[1024,768]{1,0:T(8,128)} fusion(bf16[1024,1024]{1,0:T(8,128)(2,1)} %all-gather.3.cloned.1.call-done, bf16[1024,768]{1,0:T(8,128)(2,1)} %param.19), kind=kOutput, calls=%fused_computation.75 | convolution fusion | flops 1610612736 | bytes 6815744 | tf_op jit(solution)/shard_map/dot_general | solution.py:100
  112.2 205.3 %reduce-scatter.3.cloned.1.call-done = f32[64,768]{1,0:T(8,128)} async-done(((f32[1024,768]{1,0:T(8,128)}), f32[64,768]{1,0:T(8,128)}) %reduce-scatter.3.cloned.1.call-update) | async-done | bytes 196624 | tf_op jit(solution)/shard_map/reduce_scatter | solution.py:106
  317.4 1.1 multiply_reduce_fusion
  318.5 31.1 %psum.7 = f32[64]{0:T(128)S(1)} all-reduce(f32[64]{0:T(128)S(1)} %multiply_reduce_fusion), channel_id=1, replica_groups=mesh['section'=16,'tensor'=16] {'section'}, use_global_device_ids=true, to_apply=%region_6.7 | all-reduce | flops 64 | bytes 512 | tf_op jit(solution)/shard_map/psum | solution.py:108
  349.6 1.7 multiply_convert_fusion
  351.3 74.3 %all-gather.5.cloned.1.call-done = bf16[1024,768]{1,0:T(8,128)(2,1)} async-done(((bf16[64,768]{1,0:T(8,128)(2,1)}), bf16[1024,768]{1,0:T(8,128)(2,1)}) %all-gather.5.cloned.1.call-update) | async-done | bytes 1572880 | tf_op jit(solution)/shard_map/all_gather | solution.py:114
  425.7 4.6 fusion.50
  430.3 3.0 fusion.49
  433.3 5.2 pad_maximum_fusion
  438.5 84.7 %reduce-scatter.5.cloned.1.call-done = f32[64,3328]{1,0:T(8,128)} async-done(((f32[1024,3328]{1,0:T(8,128)}), f32[64,3328]{1,0:T(8,128)}) %reduce-scatter.5.cloned.1.call-update) | async-done | bytes 851984 | tf_op jit(solution)/shard_map/reduce_scatter | solution.py:118
  523.2 2.0 slice_multiply_fusion
  (49 shorter events, 6.4 us)
Async XLA Ops:
  7.2 418.5 %copy-start = (bf16[768,1664]{1,0:T(8,128)(2,1)S(1)}, bf16[768,1664]{1,0:T(8,128)(2,1)}, u32[]{:S(2)}) copy-start(bf16[768,1664]{1,0:T(8,128)(2,1)} %param.23) | copy-start | bytes 7667716
  7.2 12.0 %copy-start.6 = (s32[64]{0:T(128)S(1)}, s32[64]{0:T(128)}, u32[]{:S(2)}) copy-start(s32[64]{0:T(128)} %param.15) | copy-start | bytes 772
  9.7 12.3 %all-to-all-start = ((s32[16,1,2]{2,1,0:T(1,128)}), s32[16,1,2]{2,1,0:T(1,128)S(1)}, u32[]{:S(2)}, u32[]{:S(2)}) async-start(s32[16,1,2]{2,1,0:T(1,128)} %bitcast.4), calls=%async_computation | async-start | bytes 16384 | tf_op jit(solution)/shard_map/all_to_all | solution.py:87
  21.3 5.9 %copy-start.5 = (s32[64,4]{0,1:T(4,128)S(1)}, s32[64,4]{0,1:T(4,128)}, u32[]{:S(2)}) copy-start(s32[64,4]{0,1:T(4,128)} %param.14) | copy-start | bytes 3076
  21.3 34.0 %copy-start.3 = (bf16[64,8,128]{2,1,0:T(8,128)(2,1)S(1)}, bf16[64,8,128]{2,1,0:T(8,128)(2,1)}, u32[]{:S(2)}) copy-start(bf16[64,8,128]{2,1,0:T(8,128)(2,1)} %param.12) | copy-start | bytes 393220
  22.0 33.3 %all-to-all-start.1 = ((bf16[16,2,128,256]{3,2,1,0:T(8,128)(2,1)}), bf16[16,2,128,256]{3,2,1,0:T(8,128)(2,1)}, u32[]{:S(2)}, u32[]{:S(2)}) async-start(bf16[16,2,128,256]{3,2,1,0:T(8,128)(2,1)} %copy.27), calls=%async_computation.1 | async-start | bytes 4194304 | tf_op jit(solution)/shard_map/all_to_all | solution.py:86
  27.2 78.9 %all-gather.3.cloned.1.call-start = ((), (), s32[]{:S(2)}) async-start(), calls=%async_computation.4 | async-start | bytes 2228224 | tf_op jit(solution)/shard_map/all_gather | solution.py:101
  65.6 251.9 %reduce-scatter.3.cloned.1.call-start = ((), (), s32[]{:S(2)}) async-start(), calls=%async_computation.5 | async-start | bytes 3342336 | tf_op jit(solution)/shard_map/reduce_scatter | solution.py:106
  111.5 0.7 copy-start.4
  111.5 206.0 %copy-start.2 = (bf16[64,768]{1,0:T(8,128)(2,1)S(1)}, bf16[64,768]{1,0:T(8,128)(2,1)}, u32[]{:S(2)}) copy-start(bf16[64,768]{1,0:T(8,128)(2,1)} %param.20) | copy-start | bytes 294916
  111.5 314.1 %all-gather.5.cloned.1.call-start = ((), (), s32[]{:S(2)}) async-start(), calls=%async_computation.6 | async-start | bytes 1671168 | tf_op jit(solution)/shard_map/all_gather | solution.py:114
  351.3 171.9 %reduce-scatter.5.cloned.1.call-start = ((), (), s32[]{:S(2)}) async-start(), calls=%async_computation.7 | async-start | bytes 14483456 | tf_op jit(solution)/shard_map/reduce_scatter | solution.py:118
  425.7 4.6 copy-start.7
  425.7 4.6 copy-start.8
  438.5 86.7 %copy-start.1 = (bf16[768,1664]{1,0:T(8,128)(2,1)S(1)}, bf16[768,1664]{1,0:T(8,128)(2,1)}, u32[]{:S(2)}) copy-start(bf16[768,1664]{1,0:T(8,128)(2,1)} %param.23) | copy-start | bytes 7667716
Sparse Core Ops, SparseCore 0:
  65.7 40.2 all-gather.2
  111.6 205.7 reduce-scatter.2
  351.4 74.2 all-gather.4
  438.7 84.5 reduce-scatter.4
where the time goes:
time: 534 us; the launch traced here: 532 us
  waiting for transfers between devices  430 us (81%)
  blocking collectives  31.1 us (6%)
  matrix products  19.2 us (4%)
  other arithmetic  18.1 us (3%)
  between operations  14 us (3%)
  starting transfers between devices  12.4 us (2%)
  local copies, waits for them, and re-layouts  7.19 us (1%)
    reduce_scatter x1, waiting for transfers between devices, body(): lax.psum_scatter(partial_proj, 'tensor', scatter_dimension=0, tiled=True)  205 us
    reduce_scatter x1, waiting for transfers between devices, body(): lax.psum_scatter(both_terms, 'section', scatter_dimension=0, tiled=True)  84.7 us
    all_gather x1, waiting for transfers between devices, body(): segment = lax.all_gather(normed, 'tensor', axis=0, tiled=True)  74.3 us
    all_gather x1, waiting for transfers between devices, body(): lax.all_gather(attention, 'section', axis=0, tiled=True)  40.2 us
    psum x1, blocking collectives, body(): squares = lax.psum(jnp.sum(combined * combined, axis=1), 'section')  31.1 us
    all_to_all x1, waiting for transfers between devices, body(): lax.all_to_all(send_blocks, 'section', split_axis=0, concat_axis=0, tiled...  24.6 us
  transfers between devices with their start and end apart: 6, of which 6 were waited for; matrix products, arithmetic and copies ran while one was open for 2% of the time, Pallas kernels for 0%

commit v1 on v0

--- a/solution.py
+++ b/solution.py
@@ -1,13 +1,475 @@
+import functools
+
 import jax
 import jax.numpy as jnp
 from jax import lax
+from jax.experimental import pallas as pl
+from jax.experimental.pallas import tpu as pltpu
 from jax.sharding import PartitionSpec as P
 
+MESH = pl.DeviceIdType.MESH
 CAP = 2
-
-
 NEG_LARGE = -1e30
 EPSILON = 1e-05
+VMEM_LIMIT = 60 * 1024 * 1024
+BF = jnp.bfloat16
+F32 = jnp.float32
+
+
+def coords():
+    s = lax.axis_index("section")
+    t = lax.axis_index("tensor")
+    return s, t
+
+
+def section_of(x, y, core):
+    return x * 8 + y * 2 + core
+
+
+def remote(src, dst, ssem, rsem, dev):
+    return pltpu.make_async_remote_copy(
+        src_ref=src, dst_ref=dst, send_sem=ssem, recv_sem=rsem,
+        device_id=dev, device_id_type=MESH)
+
+
+def signal(sem, dev):
+    pl.semaphore_signal(sem, inc=1, device_id=dev, device_id_type=MESH)
+
+
+def proj_kernel(att, wo, res, gain, proj_out, mg_out, sq_out,
+                pz, rbuf, sbuf, xs, xr,
+                rs_send, rs_recv, x_send, x_recv, ag_send, ag_recv, agx_send, agx_recv):
+    s, t = coords()
+    xh, z = t // 8, t % 8
+    peer = (s, (1 - xh) * 8 + z)
+    right = (s, xh * 8 + (z + 1) % 8)
+    left = (s, xh * 8 + (z + 7) % 8)
+    ways = (right, left)
+    barrier = pltpu.get_barrier_semaphore()
+    for dev in (right, left, peer):
+        signal(barrier, dev)
+    rows = res.shape[0]
+
+    def compute(slot, off):
+        zz = (z + off) % 8
+        a = jnp.concatenate([att[pl.ds(pl.multiple_of(zz * rows, rows), rows), :],
+                             att[pl.ds(pl.multiple_of((8 + zz) * rows, rows), rows), :]], 0)
+        p = jnp.dot(a, wo[...], preferred_element_type=F32)
+        pz[slot, 0] = p[:rows]
+        pz[slot, 1] = p[rows:]
+
+    def off_of(slot):
+        k = (slot + 1) // 2
+        plus = slot % 2 == 1
+        return jnp.where(plus, 4 - k, 4 + k) % 8
+
+    def slot_of(way, k):
+        return 0 if k == 0 else 2 * k - 1 + way
+
+    def rs(way, k, h):
+        return remote(sbuf.at[way, k, h], rbuf.at[way, k, h],
+                      rs_send.at[way, k, h], rs_recv.at[way, k, h], ways[way])
+
+    def send(way, k, h, add):
+        v = pz[slot_of(way, k), h]
+        if add:
+            rs(way, k - 1, h).wait_recv()
+            v = v + rbuf[way, k - 1, h].astype(F32)
+        sbuf[way, k, h] = v.astype(BF)
+        rs(way, k, h).start()
+
+    compute(0, 4)
+    pl.semaphore_wait(barrier, 3)
+    for way in (0, 1):
+        send(way, 0, way, False)
+
+    def group(lo, hi):
+        @pl.loop(lo, hi)
+        def _(i):
+            compute(i, off_of(i))
+
+    group(1, 3)
+    for way in (0, 1):
+        send(way, 1, 1 - way, False)
+    group(3, 8)
+    for k in (1, 2, 3):
+        for way in (0, 1):
+            if k == 1:
+                send(way, 1, way, True)
+            else:
+                send(way, k, 1 - way, True)
+        if k > 1:
+            for way in (0, 1):
+                send(way, k, way, True)
+
+    def total(h):
+        for way in (0, 1):
+            rs(way, 3, h).wait_recv()
+        return pz[7, h] + rbuf[0, 3, h].astype(F32) + rbuf[1, 3, h].astype(F32)
+
+    def xcopy():
+        return remote(xs, xr, x_send, x_recv, peer)
+
+    xs[...] = total(1 - xh).astype(BF)
+    xcopy().start()
+    proj_out[...] = total(xh)
+    xcopy().wait_recv()
+    proj = proj_out[...] + xr[...].astype(F32)
+    proj_out[...] = proj
+    mixed = proj + res[...].astype(F32)
+    own = xh * 8 + z
+    mg_out[own] = (mixed * gain[...].astype(F32)).astype(BF)
+
+    def agx():
+        return remote(mg_out.at[own], mg_out.at[own], agx_send, agx_recv, peer)
+
+    def ag(way, k, h):
+        hh = xh if h == 0 else 1 - xh
+        zz = (z - k + 8) % 8 if way == 0 else (z + k) % 8
+        blk = hh * 8 + zz
+        return remote(mg_out.at[blk], mg_out.at[blk], ag_send.at[way, k, h], ag_recv.at[way, k, h], ways[way])
+
+    for way in (0, 1):
+        ag(way, 0, 0).start()
+    agx().start()
+    sq_out[...] = jnp.sum(mixed * mixed, axis=1, keepdims=True) + jnp.zeros(sq_out.shape, F32)
+    agx().wait_recv()
+    for way in (0, 1):
+        ag(way, 0, 1).start()
+    for k in (1, 2):
+        for h in (0, 1):
+            for way in (0, 1):
+                ag(way, k - 1, h).wait_recv()
+                ag(way, k, h).start()
+    def ag_last(way):
+        blk = way * 8 + ((z + 5) % 8 if way == 0 else (z + 3) % 8)
+        return remote(mg_out.at[blk], mg_out.at[blk], ag_send.at[way, 3, 0], ag_recv.at[way, 3, 0], ways[way])
+
+    for way in (0, 1):
+        for h in (0, 1):
+            ag(way, 2, h).wait_recv()
+        ag_last(way).start()
+    for way in (0, 1):
+        ag_last(way).wait_recv()
+        ag_last(way).wait_send()
+    for way in (0, 1):
+        for k in range(4):
+            for h in (0, 1):
+                if k == 0 and h != way:
+                    continue
+                rs(way, k, h).wait_send()
+        for k in range(3):
+            for h in (0, 1):
+                ag(way, k, h).wait_send()
+    xcopy().wait_send()
+    agx().wait_send()
+
+
+def proj_call(att, wo, res, gain):
+    rows, width = res.shape
+    dma = pltpu.SemaphoreType.DMA
+    vm = pl.BlockSpec(memory_space=pltpu.VMEM)
+    return pl.pallas_call(
+        proj_kernel,
+        out_shape=(jax.ShapeDtypeStruct((rows, width), F32),
+                   jax.ShapeDtypeStruct((16, rows, width), BF),
+                   jax.ShapeDtypeStruct((rows, 128), F32)),
+        in_specs=[vm] * 4,
+        out_specs=(vm,) * 3,
+        scratch_shapes=[
+            pltpu.VMEM((8, 2, rows, width), F32),
+            pltpu.VMEM((2, 4, 2, rows, width), BF),
+            pltpu.VMEM((2, 4, 2, rows, width), BF),
+            pltpu.VMEM((rows, width), BF),
+            pltpu.VMEM((rows, width), BF),
+            dma((2, 4, 2)), dma((2, 4, 2)), dma, dma,
+            dma((2, 4, 2)), dma((2, 4, 2)), dma, dma,
+        ],
+        compiler_params=pltpu.CompilerParams(
+            collective_id=1, has_side_effects=True, vmem_limit_bytes=VMEM_LIMIT),
+        name="projection",
+    )(att, wo, res, gain)
+
+
+def ffn_kernel(mg, gate, up, sq, hid,
+               wf, mgf, pb, pa, bs, br, as_, ar, xas, xar, xbs, xbr, ps, pr, sqr, fin,
+               w_sem, m_sem, ws, wr, ms, mr,
+               bss, brs, ass, ars, xass, xars, xbss, xbrs, pss, prs, sqs, sqrs, dgs, dgr):
+    s, t = coords()
+    x, y, core = s // 8, (s // 2) % 4, s % 2
+    mate = (section_of(x, y, 1 - core), t)
+    xpeer = (section_of(1 - x, y, core), t)
+    yp = (section_of(x, (y + 1) % 4, core), t)
+    ym = (section_of(x, (y + 3) % 4, core), t)
+    ways = (yp, ym)
+    diag = s == t
+    n = 16
+    FFN = gate.shape[1]
+    CA = xar.shape[2]
+    CB = FFN - CA
+    H = CA // 2
+    R = 128
+    width = gate.shape[0]
+    barrier = pltpu.get_barrier_semaphore()
+    for dev in (mate, xpeer, yp, ym):
+        signal(barrier, dev)
+
+    @pl.when(diag)
+    def _():
+        for i in range(1, n):
+            signal(barrier, ((s + i) % n, t))
+
+    @pl.when(jnp.logical_not(diag))
+    def _():
+        signal(barrier, (s, s))
+
+    def w_own(c):
+        return pltpu.make_async_copy(gate if c == 0 else up, wf.at[c], w_sem)
+
+    def m_own():
+        return pltpu.make_async_copy(mg, mgf.at[core], m_sem)
+
+    for c in (0, 1):
+        @pl.when(core == c)
+        def _():
+            w_own(c).start()
+    m_own().start()
+
+    @pl.when(diag)
+    def _():
+        pl.semaphore_wait(barrier, 4 + n - 1)
+
+    @pl.when(jnp.logical_not(diag))
+    def _():
+        pl.semaphore_wait(barrier, 5)
+
+    def w_far(c):
+        return remote(up if c == 0 else gate, wf.at[c], ws, wr, mate)
+
+    def m_far():
+        return remote(mg, mgf.at[core], ms, mr, mate)
+
+    m_far().start()
+    for c in (0, 1):
+        @pl.when(core == c)
+        def _():
+            w_far(c).start()
+
+    def sq_copy(slot):
+        return remote(sq, sqr.at[slot], sqs, sqrs.at[slot], (t, t))
+
+    def dg_copy(i):
+        return remote(fin, fin, dgs.at[i], dgr, (s, (t + i) % n))
+
+    @pl.when(jnp.logical_not(diag))
+    def _():
+        sq_copy((s - t + n) % n).start()
+
+    for c in (0, 1):
+        @pl.when(core == c)
+        def _():
+            w_own(c).wait()
+    m_own().wait()
+    m_far().wait_recv()
+    for c in (0, 1):
+        @pl.when(core == c)
+        def _():
+            w_far(c).wait_recv()
+
+    def part(xx, yy, c0, cn):
+        r0 = pl.multiple_of((xx * 4 + yy) * R, R)
+        return (jnp.dot(mgf[0, pl.ds(r0, R), :], wf[0, :, c0:c0 + cn], preferred_element_type=F32)
+                + jnp.dot(mgf[1, pl.ds(r0, R), :], wf[1, :, c0:c0 + cn], preferred_element_type=F32))
+
+    def yoff(k):
+        return (y + jnp.where(k == 0, 2, jnp.where(k == 1, 1, jnp.where(k == 2, 3, 0)))) % 4
+
+    def b_group(lo, hi):
+        @pl.loop(lo, hi)
+        def _(i):
+            pb[i] = part(i % 2, yoff(i // 2), CA, CB)
+
+    def a_group(xx, base, lo, hi):
+        @pl.loop(lo, hi)
+        def _(i):
+            pa[base + i] = part(xx, yoff(i), 0, CA)
+
+    def bcopy(way, m):
+        return remote(bs.at[way, m], br.at[way, m], bss.at[way, m], brs.at[way, m], ways[way])
+
+    def acopy(way, m):
+        return remote(as_.at[way, m], ar.at[way, m], ass.at[way, m], ars.at[way, m], ways[way])
+
+    def xacopy(k):
+        return remote(xas.at[k], xar.at[k], xass.at[k], xars.at[k], xpeer)
+
+    def xbcopy():
+        return remote(xbs, xbr, xbss, xbrs, xpeer)
+
+    def xa_send(k):
+        xas[k] = pa[4 + k].astype(BF)
+        xacopy(k).start()
+
+    b_group(0, 2)
+    for way in (0, 1):
+        bs[way, 0] = pb[way].astype(BF)
+        bcopy(way, 0).start()
+    a_group(1 - x, 4, 0, 1)
+    xa_send(0)
+    b_group(2, 6)
+    for way in (0, 1):
+        bs[way, 1] = pb[2 * (1 + way) + 1 - way].astype(BF)
+        bcopy(way, 1).start()
+    a_group(1 - x, 4, 1, 4)
+    for k in (1, 2, 3):
+        xa_send(k)
+    for way in (0, 1):
+        bcopy(way, 0).wait_recv()
+        bs[way, 2] = (pb[2 * (1 + way) + way] + br[way, 0].astype(F32)).astype(BF)
+        bcopy(way, 2).start()
+    a_group(x, 0, 0, 4)
+    b_group(6, 8)
+
+    def a_sum(k):
+        xacopy(k).wait_recv()
+        pa[k] = pa[k] + xar[k].astype(F32)
+
+    a_sum(0)
+    for way in (0, 1):
+        as_[way, 0] = pa[0, :, way * H:(way + 1) * H].astype(BF)
+        acopy(way, 0).start()
+    for k in (1, 2):
+        a_sum(k)
+        way = k - 1
+        as_[way, 1] = pa[k, :, (1 - way) * H:(2 - way) * H].astype(BF)
+        acopy(way, 1).start()
+    for way in (0, 1):
+        acopy(way, 0).wait_recv()
+        as_[way, 2] = (pa[1 + way, :, way * H:(way + 1) * H] + ar[way, 0].astype(F32)).astype(BF)
+        acopy(way, 2).start()
+
+    for way in (0, 1):
+        bcopy(way, 1).wait_recv()
+        bcopy(way, 2).wait_recv()
+    for h in (0, 1):
+        pb[6 + h] = pb[6 + h] + br[h, 2].astype(F32) + br[1 - h, 1].astype(F32)
+    xbs[...] = pb[6 + 1 - x].astype(BF)
+    xbcopy().start()
+
+    @pl.when(diag)
+    def _():
+        acc = sq[...]
+        for i in range(1, n):
+            sq_copy(i).wait_recv()
+            acc = acc + sqr[i]
+        fin[...] = acc
+        for i in range(1, n):
+            dg_copy(i).start()
+
+    a_sum(3)
+    for way in (0, 1):
+        acopy(way, 1).wait_recv()
+        acopy(way, 2).wait_recv()
+    for h in (0, 1):
+        pa[3, :, h * H:(h + 1) * H] = (pa[3, :, h * H:(h + 1) * H]
+                                       + ar[h, 2].astype(F32) + ar[1 - h, 1].astype(F32))
+
+    HR = R // 2
+    give = pl.multiple_of((1 - core) * HR, HR)
+    keep = pl.multiple_of(core * HR, HR)
+
+    def pcopy(i):
+        return remote(ps.at[i], pr.at[i], pss.at[i], prs.at[i], mate)
+
+    ps[0, :, :CA] = pa[3, pl.ds(give, HR), :]
+    pcopy(0).start()
+    xbcopy().wait_recv()
+    own = pb[6 + x] + xbr[...].astype(F32)
+    pb[6] = own
+    ps[1, :, :CB] = pb[6, pl.ds(give, HR), :]
+    pcopy(1).start()
+
+    @pl.when(jnp.logical_not(diag))
+    def _():
+        dg_copy(1).wait_recv()
+
+    inv = lax.rsqrt(fin[:, :1] / (width * n) + EPSILON)
+
+    def finish(i, mine, c0, cn):
+        pcopy(i).wait_recv()
+        other = pr[i, :, :cn] * inv
+        mine = mine * inv
+        g = jnp.where(core == 0, mine, other)
+        u = jnp.where(core == 0, other, mine)
+        hid[:, c0:c0 + cn] = g / (1.0 + jnp.exp(-g)) * u
+
+    finish(0, pa[3, pl.ds(keep, HR), :], 0, CA)
+    finish(1, pb[6, pl.ds(keep, HR), :], CA, CB)
+
+    for way in (0, 1):
+        for m in (0, 1, 2):
+            bcopy(way, m).wait_send()
+            acopy(way, m).wait_send()
+    for k in range(4):
+        xacopy(k).wait_send()
+    xbcopy().wait_send()
+    for i in (0, 1):
+        pcopy(i).wait_send()
+    m_far().wait_send()
+    for c in (0, 1):
+        @pl.when(core == c)
+        def _():
+            w_far(c).wait_send()
+
+    @pl.when(diag)
+    def _():
+        for i in range(1, n):
+            dg_copy(i).wait_send()
+
+    @pl.when(jnp.logical_not(diag))
+    def _():
+        sq_copy((s - t + n) % n).wait_send()
+
+
+def ffn_call(mg, gate, up, sq):
+    width, ffn = gate.shape
+    rows = sq.shape[0]
+    ca = 6 * 128
+    cb = ffn - ca
+    dma = pltpu.SemaphoreType.DMA
+    vm = pl.BlockSpec(memory_space=pltpu.VMEM)
+    hbm = pl.BlockSpec(memory_space=pl.ANY)
+    return pl.pallas_call(
+        ffn_kernel,
+        out_shape=jax.ShapeDtypeStruct((rows, ffn), F32),
+        in_specs=[hbm, hbm, hbm, vm],
+        out_specs=vm,
+        scratch_shapes=[
+            pltpu.VMEM((2, width, ffn), BF),
+            pltpu.VMEM((2, 16 * rows, width), BF),
+            pltpu.VMEM((8, 128, cb), F32),
+            pltpu.VMEM((8, 128, ca), F32),
+            pltpu.VMEM((2, 3, 128, cb), BF),
+            pltpu.VMEM((2, 3, 128, cb), BF),
+            pltpu.VMEM((2, 3, 128, ca // 2), BF),
+            pltpu.VMEM((2, 3, 128, ca // 2), BF),
+            pltpu.VMEM((4, 128, ca), BF),
+            pltpu.VMEM((4, 128, ca), BF),
+            pltpu.VMEM((128, cb), BF),
+            pltpu.VMEM((128, cb), BF),
+            pltpu.VMEM((2, 64, cb), F32),
+            pltpu.VMEM((2, 64, cb), F32),
+            pltpu.VMEM((16, rows, 128), F32),
+            pltpu.VMEM((rows, 128), F32),
+            dma, dma, dma, dma, dma, dma,
+            dma((2, 3)), dma((2, 3)), dma((2, 3)), dma((2, 3)),
+            dma((4,)), dma((4,)), dma, dma, dma((2,)), dma((2,)),
+            dma, dma((16,)), dma((16,)), dma,
+        ],
+        compiler_params=pltpu.CompilerParams(
+            collective_id=2, has_side_effects=True, vmem_limit_bytes=VMEM_LIMIT),
+        name="ffn",
+    )(mg, gate, up, sq)
 
 
 def cached_allowed(table_rows, lengths, slot_count, block_len):
@@ -97,27 +559,9 @@
         jnp.concatenate([pool_allowed, new_allowed], 1),
     )
     attention = (summed / totals[:, :, None]).astype(jnp.bfloat16).reshape(row_count, -1)
-    partial_proj = jnp.dot(
-        lax.all_gather(attention, "section", axis=0, tiled=True),
-        out_weight,
-        preferred_element_type=jnp.float32,
-    )
-    model_width = residual.shape[1] * sections
-    attn_proj = lax.psum_scatter(partial_proj, "tensor", scatter_dimension=0, tiled=True)
-    combined = residual.astype(jnp.float32) + attn_proj
-    squares = lax.psum(jnp.sum(combined * combined, axis=1), "section")
-    normed = (
-        combined
-        * norm_gain.astype(jnp.float32)[None, :]
-        * lax.rsqrt(squares / model_width + EPSILON)[:, None]
-    ).astype(jnp.bfloat16)
-    segment = lax.all_gather(normed, "tensor", axis=0, tiled=True)
-    gate_part = jnp.dot(segment, gate_weight, preferred_element_type=jnp.float32)
-    up_part = jnp.dot(segment, up_weight, preferred_element_type=jnp.float32)
-    both_terms = jnp.concatenate([gate_part, up_part], 1)
-    gate_up = lax.psum_scatter(both_terms, "section", scatter_dimension=0, tiled=True)
-    hidden_units = gate_weight.shape[1]
-    hidden = jax.nn.silu(gate_up[:, :hidden_units]) * gate_up[:, hidden_units:]
+    att = lax.all_gather(attention, "section", axis=0, tiled=True)
+    attn_proj, mg, sq = proj_call(att, out_weight, residual, norm_gain.reshape(1, -1))
+    hidden = ffn_call(mg.reshape(-1, mg.shape[2]), gate_weight, up_weight, sq)
     return (attn_proj, hidden)
 
 

time: 534 us -> 209 us (0.39)
  waiting for transfers between devices: 430 us -> 65.9 us
  Pallas kernels: 0 us -> 93.2 us
  blocking collectives: 31.1 us -> 0 us
  matrix products: 19.2 us -> 6.11 us
  other arithmetic: 18.1 us -> 8.14 us
    reduce_scatter x2 -> x0, waiting for transfers between devices: 290 us -> none  [the longest x1 205 us: body(): lax.psum_scatter(partial_proj, 'tensor', scatter_dimension=0, tiled=True)]
    pallas_call x0 -> x2, Pallas kernels: none -> 93.2 us  [the longest x1 47.1 us: proj_call(): pl.pallas_call(proj_kernel, out_shape=(jax.ShapeDtypeStruct((rows, width)...]
    all_gather x2 -> x1, waiting for transfers between devices: 115 us -> 39.9 us  [body(): att = lax.all_gather(attention, 'section', axis=0, tiled=True)]
    psum x1 -> x0, blocking collectives: 31.1 us -> none  [body(): squares = lax.psum(jnp.sum(combined * combined, axis=1), 'section')]
    dot_general x3 -> x0, matrix products: 13.1 us -> none  [the longest x1 5.48 us: body(): jnp.dot(lax.all_gather(attention, 'section', axis=0, tiled=True), out_wei...]
  transfers between devices with their start and end apart: 6 -> 3, of which waited for: 6 -> 3; matrix products, arithmetic and copies ran while one was open for 2% -> 4% of each run, Pallas kernels for 0% -> 0%
where the time goes in v1:
time: 209 us
  Pallas kernels  93.2 us (45%)
  waiting for transfers between devices  65.9 us (32%)
  between operations  14.2 us (7%)
  starting transfers between devices  12.3 us (6%)
  local copies, waits for them, and re-layouts  8.67 us (4%)
  other arithmetic  8.14 us (4%)
  matrix products  6.11 us (3%)
    pallas_call x1, Pallas kernels, proj_call(): pl.pallas_call(proj_kernel, out_shape=(jax.ShapeDtypeStruct((rows, width)...  47.1 us
    pallas_call x1, Pallas kernels, ffn_call(): pl.pallas_call(ffn_kernel, out_shape=jax.ShapeDtypeStruct((rows, ffn), F3...  46.1 us
    all_gather x1, waiting for transfers between devices, body(): att = lax.all_gather(attention, 'section', axis=0, tiled=True)  39.9 us
    all_to_all x1, waiting for transfers between devices, body(): lax.all_to_all(send_blocks, 'section', split_axis=0, concat_axis=0, tiled...  25.3 us
    all_to_all x1, starting transfers between devices, body(): lax.all_to_all(send_rows, 'section', split_axis=0, concat_axis=0, tiled=T...  6.91 us
    all_to_all x1, starting transfers between devices, body(): lax.all_to_all(send_blocks, 'section', split_axis=0, concat_axis=0, tiled...  5.16 us
    sub x1, other arithmetic, partial_softmax(): weights = jnp.where(token_mask, jnp.exp(masked - highest[:, :, None]), 0.0)  4.32 us
  transfers between devices with their start and end apart: 3, of which 3 were waited for; matrix products, arithmetic and copies ran while one was open for 4% of the time, Pallas kernels for 0%

profile of v1, /device:TPU:1, one launch (start us, length us, event | category | flops | bytes accessed | tf_op | source)
XLA Modules:
  0.0 208.6 jit_solution(4472179587224294581)
XLA Ops:
  7.2 1.0 convert_reduce_fusion
  8.2 0.7 multiply_add_fusion.1
  9.0 0.7 sub.34
  9.7 6.9 %all-to-all-start = ((s32[16,1,2]{2,1,0:T(1,128)}), s32[16,1,2]{2,1,0:T(1,128)S(1)}, u32[]{:S(2)}, u32[]{:S(2)}) async-start(s32[16,1,2]{2,1,0:T(1,128)} %bitcast.4), calls=%async_computation | async-start | bytes 16384 | tf_op jit(solution)/shard_map/all_to_all | solution.py:549
  16.6 0.7 broadcast_add_fusion.4
  17.3 1.1 dynamic-slice_bitcast_fusion
  18.3 0.8 fusion.35
  19.3 2.0 copy.24
  21.3 0.7 all-to-all-done
  22.0 5.2 %all-to-all-start.1 = ((bf16[16,2,128,256]{3,2,1,0:T(8,128)(2,1)}), bf16[16,2,128,256]{3,2,1,0:T(8,128)(2,1)}, u32[]{:S(2)}, u32[]{:S(2)}) async-start(bf16[16,2,128,256]{3,2,1,0:T(8,128)(2,1)} %copy.24), calls=%async_computation.1 | async-start | bytes 4194304 | tf_op jit(solution)/shard_map/all_to_all | solution.py:548
  27.7 0.3 and_or_fusion
  28.1 0.5 broadcast.182
  28.6 0.7 reduce.3
  29.9 25.3 %all-to-all-done.1 = bf16[16,2,128,256]{3,2,1,0:T(8,128)(2,1)} async-done(((bf16[16,2,128,256]{3,2,1,0:T(8,128)(2,1)}), bf16[16,2,128,256]{3,2,1,0:T(8,128)(2,1)}, u32[]{:S(2)}, u32[]{:S(2)}) %all-to-all-start.1) | async-done | bytes 2097184 | tf_op jit(solution)/shard_map/all_to_all | solution.py:548
  55.2 2.6 %fusion.14 = f32[4608,64,8]{0,1,2:T(8,128)S(1)} fusion(bf16[512,256]{1,0:T(8,128)(2,1)S(1)} %bitcast.62, bf16[4096,256]{1,0:T(8,128)(2,1)} %bitcast.11, bf16[64,8,128]{2,1,0:T(8,128)(2,1)S(1)} %copy-done.2), kind=kOutput, calls=%fused_computation.17 | convolution fusion | flops 606339072 | bytes 11927552 | tf_op jit(solution)/shard_map/rhd,kd->rhk/dot_general | solution.py:488
  57.9 4.3 %fusion.2 = (f32[64,8]{0,1:T(8,128)S(1)}, f32[64,8,4608]{2,0,1:T(8,128)S(1)}) fusion(pred[64,4608]{1,0:T(8,128)(4,1)S(1)} %pad_add_fusion, f32[4608,64,8]{0,1,2:T(8,128)S(1)} %fusion.14), kind=kOutput, calls=%fused_computation.4 | output fusion | flops 11801087 | bytes 19171328 | tf_op jit(solution)/shard_map/sub | solution.py:494
  62.2 2.7 %fusion.29 = bf16[8,8,8,128]{3,2,1,0:T(8,128)(2,1)S(1)} fusion(bf16[4096,256]{1,0:T(8,128)(2,1)} %bitcast.11, bf16[512,256]{1,0:T(8,128)(2,1)S(1)} %bitcast.63, f32[64,8,4608]{2,0,1:T(8,128)S(1)} %get-tuple-element.16, pred[64,4608]{1,0:T(8,128)(4,1)S(1)} %pad_add_fusion, f32[64,8]{0,1:T(8,128)S(1)} %get-tuple-element.15), kind=kOutput, calls=%fused_computation.24 | convolution fusion | flops 611188736 | bytes 12224512 | tf_op jit(solution)/shard_map/rhk,kd->rhd/dot_general | solution.py:496
  64.9 0.7 copy.42
  65.6 0.6 reshape.269.gain
  66.2 39.9 %all-gather.2.cloned.1.call-done.att = bf16[1024,1024]{1,0:T(8,128)(2,1)} async-done(((bf16[64,1024]{1,0:T(8,128)(2,1)}), bf16[1024,1024]{1,0:T(8,128)(2,1)}) %all-gather.2.cloned.1.call-update) | async-done | bytes 2097168 | tf_op jit(solution)/shard_map/all_gather | solution.py:562
  106.0 47.1 %projection.1 = (f32[64,768]{1,0:T(8,128)}, bf16[16,64,768]{2,1,0:T(8,128)(2,1)}, f32[64,128]{1,0:T(8,128)}) custom-call(bf16[1024,1024]{1,0:T(8,128)(2,1)} %all-gather.2.cloned.1.call-done.att, bf16[1024,768]{1,0:T(8,128)(2,1)} %wo.1, bf16[64,768]{1,0:T(8,128)(2,1)} %res.1, bf16[1,768]{1,0:T(2,128)(2,1)} %reshape.269.gain), custom_call_target="tpu_custom_call" | custom-call | tf_op jit(solution)/shard_map/projection/pallas_call | solution.py:172
  153.1 46.1 %ffn.1 = f32[64,1664]{1,0:T(8,128)} custom-call(bf16[1024,768]{1,0:T(8,128)(2,1)} %bitcast.61, bf16[768,1664]{1,0:T(8,128)(2,1)} %gate.1, bf16[768,1664]{1,0:T(8,128)(2,1)} %up.1, f32[64,128]{1,0:T(8,128)} %get-tuple-element.7.sq), custom_call_target="tpu_custom_call" | custom-call | tf_op jit(solution)/shard_map/ffn/pallas_call | solution.py:442
  199.3 0.7 copy.46
  200.0 1.8 copy.47
  (29 shorter events, 1.3 us)
Async XLA Ops:
  7.2 20.9 %copy-start = (bf16[8,4,128,256]{3,2,1,0:T(8,128)(2,1)S(1)}, bf16[8,4,128,256]{3,2,1,0:T(8,128)(2,1)}, u32[]{:S(2)}) copy-start(bf16[8,4,128,256]{3,2,1,0:T(8,128)(2,1)} %param.13) | copy-start | bytes 6291460
  7.2 12.0 %copy-start.5 = (s32[64]{0:T(128)S(1)}, s32[64]{0:T(128)}, u32[]{:S(2)}) copy-start(s32[64]{0:T(128)} %param.15) | copy-start | bytes 772
  9.7 12.3 %all-to-all-start = ((s32[16,1,2]{2,1,0:T(1,128)}), s32[16,1,2]{2,1,0:T(1,128)S(1)}, u32[]{:S(2)}, u32[]{:S(2)}) async-start(s32[16,1,2]{2,1,0:T(1,128)} %bitcast.4), calls=%async_computation | async-start | bytes 16384 | tf_op jit(solution)/shard_map/all_to_all | solution.py:549
  21.3 6.1 %copy-start.3 = (s32[64,4]{0,1:T(4,128)S(1)}, s32[64,4]{0,1:T(4,128)}, u32[]{:S(2)}) copy-start(s32[64,4]{0,1:T(4,128)} %param.14) | copy-start | bytes 3076
  21.3 34.0 %copy-start.2 = (bf16[64,8,128]{2,1,0:T(8,128)(2,1)S(1)}, bf16[64,8,128]{2,1,0:T(8,128)(2,1)}, u32[]{:S(2)}) copy-start(bf16[64,8,128]{2,1,0:T(8,128)(2,1)} %param.12) | copy-start | bytes 393220
  22.0 33.3 %all-to-all-start.1 = ((bf16[16,2,128,256]{3,2,1,0:T(8,128)(2,1)}), bf16[16,2,128,256]{3,2,1,0:T(8,128)(2,1)}, u32[]{:S(2)}, u32[]{:S(2)}) async-start(bf16[16,2,128,256]{3,2,1,0:T(8,128)(2,1)} %copy.24), calls=%async_computation.1 | async-start | bytes 4194304 | tf_op jit(solution)/shard_map/all_to_all | solution.py:548
  27.1 78.9 %all-gather.2.cloned.1.call-start = ((), (), s32[]{:S(2)}) async-start(), calls=%async_computation.2 | async-start | bytes 2228224 | tf_op jit(solution)/shard_map/all_gather | solution.py:562
  62.2 3.4 %copy-start.4 = (bf16[768]{0:T(1024)(128)(2,1)S(1)}, bf16[768]{0:T(1024)(128)(2,1)}, u32[]{:S(2)}) copy-start(bf16[768]{0:T(1024)(128)(2,1)} %param.21) | copy-start | bytes 4612
  153.1 46.2 %copy-start.1 = (f32[64,768]{1,0:T(8,128)S(1)}, f32[64,768]{1,0:T(8,128)}, u32[]{:S(2)}) copy-start(f32[64,768]{1,0:T(8,128)} %get-tuple-element.29) | copy-start | bytes 589828
Sparse Core Ops, SparseCore 0:
  65.7 40.2 all-gather.1

commit v2 on v1

--- a/solution.py
+++ b/solution.py
@@ -472,34 +472,209 @@
     )(mg, gate, up, sq)
 
 
-def cached_allowed(table_rows, lengths, slot_count, block_len):
-    positions = jnp.arange(block_len)
-    slot_ids = jnp.arange(slot_count)
-    allowed = jnp.zeros((table_rows.shape[0], slot_count, block_len), dtype=bool)
-    for column in range(table_rows.shape[1]):
-        listed = table_rows[:, column][:, None] == slot_ids[None, :]
-        inside = positions[None, :] < (lengths - column * block_len)[:, None]
-        allowed = allowed | listed[:, :, None] & inside[:, None, :]
-    return allowed.reshape(table_rows.shape[0], slot_count * block_len)
-
-
-def partial_softmax(queries, tokens, allowed):
-    head_dim = queries.shape[2]
-    scores = jnp.einsum(
-        "rhd,kd->rhk", queries, tokens[:, :head_dim], preferred_element_type=jnp.float32
-    ) * head_dim ** (-0.5)
-    token_mask = allowed[:, None, :]
-    masked = jnp.where(token_mask, scores, NEG_LARGE)
-    highest = jnp.max(masked, axis=2)
-    weights = jnp.where(token_mask, jnp.exp(masked - highest[:, :, None]), 0.0)
-    totals = jnp.sum(weights, axis=2)
-    summed = jnp.einsum(
-        "rhk,kd->rhd",
-        weights.astype(jnp.bfloat16),
-        tokens[:, head_dim:],
-        preferred_element_type=jnp.float32,
-    )
-    return (highest, totals, summed)
+def softmax_parts(q, k, v, allowed):
+    s = lax.dot_general(q, k, (((1,), (1,)), ((), ())), preferred_element_type=F32) * (q.shape[1] ** -0.5)
+    s = jnp.where(allowed, s, NEG_LARGE)
+    m = jnp.max(s, axis=1, keepdims=True)
+    p = jnp.where(allowed, jnp.exp(s - m), 0.0)
+    l = jnp.sum(p, axis=1, keepdims=True)
+    o = jnp.dot(p.astype(BF), v, preferred_element_type=F32)
+    return m, l, o
+
+
+def attn_kernel(sec, row, q, tab, pool, arr, att,
+                kvp, kva, tb, tr, qs, qr, rb, rr, om, acc,
+                l_sem, t_s, t_r, q_s, q_r, r_s, r_r, y_s, y_r, c_s, c_r):
+    s, t = coords()
+    n = 16
+    grp = t // 2
+    HD = q.shape[1]
+    rows = tab.shape[0]
+    heads = q.shape[0] // rows
+    M = CAP * heads
+    barrier = pltpu.get_barrier_semaphore()
+
+    @pl.loop(1, n)
+    def _(i):
+        signal(barrier, ((s + i) % n, t))
+
+    pool_copy = pltpu.make_async_copy(pool.at[grp], kvp, l_sem.at[0])
+    arr_copy = pltpu.make_async_copy(arr.at[grp], kva, l_sem.at[1])
+    pool_copy.start()
+    arr_copy.start()
+
+    i2 = lax.broadcasted_iota(jnp.int32, (n * M, 128), 0)
+    slot = i2 // heads
+    head = i2 % heads
+    secs = [sec[e] for e in range(sec.shape[0])]
+    targets = []
+    for e, d in enumerate(secs):
+        rank = sum([(secs[p] == d).astype(jnp.int32) for p in range(e)], jnp.int32(0))
+        targets.append(d * CAP + rank)
+    ids = jnp.full((n * M, 128), -1, jnp.int32)
+    for e, target in enumerate(targets):
+        ids = jnp.where(slot == target, row[e] * heads + head, ids)
+    tb[...] = ids.reshape(n, M, 128)
+
+    def exchange(src, dst, ss, rs, i):
+        d = (s + i) % n
+        return remote(src.at[d], dst.at[s], ss.at[i], rs.at[i], (d, t))
+
+    def start_all(src, dst, ss, rs):
+        @pl.loop(1, n)
+        def _(i):
+            exchange(src, dst, ss, rs, i).start()
+
+    def wait_all(src, dst, ss, rs):
+        @pl.loop(1, n)
+        def _(i):
+            exchange(src, dst, ss, rs, i).wait_recv()
+
+    pl.semaphore_wait(barrier, n - 1)
+    start_all(tb, tr, t_s, t_r)
+    tr[s] = tb[s]
+
+    pool_copy.wait()
+    lane = lax.broadcasted_iota(jnp.int32, (rows, 128), 1)
+    lens = tab[:, 4:5]
+    ok = []
+    for b in range(kvp.shape[0]):
+        limit = jnp.zeros((rows, 1), jnp.int32)
+        for j in range(4):
+            limit = jnp.maximum(limit, jnp.where(tab[:, j:j + 1] == b, lens - j * 128, 0))
+        ok.append((lane < limit).astype(F32))
+    ok = jnp.concatenate(ok, axis=1)
+    ok = jnp.broadcast_to(ok[:, None, :], (rows, heads, ok.shape[1])).reshape(rows * heads, -1)
+    kv = kvp[...].reshape(-1, 2 * HD)
+
+    wait_all(tb, tr, t_s, t_r)
+    ids = tr[...].reshape(n * M, 128)
+    lane2 = lax.broadcasted_iota(jnp.int32, (n * M, 128), 1)
+    pick = jnp.concatenate([(ids == lane2 + 128 * c).astype(F32) for c in range(q.shape[0] // 128)], axis=1)
+    qs[...] = jnp.dot(pick.astype(BF), q[...], preferred_element_type=F32).astype(BF).reshape(n, M, HD)
+    start_all(qs, qr, q_s, q_r)
+    qr[s] = qs[s]
+
+    m_p, l_p, o_p = softmax_parts(q[...], kv[:, :HD], kv[:, HD:], ok > 0.5)
+    om[...] = o_p
+
+    arr_copy.wait()
+    kv = kva[...].reshape(-1, 2 * HD)
+    allowed = jnp.concatenate([(slot == target).astype(F32) for target in targets], axis=1)
+    wait_all(qs, qr, q_s, q_r)
+    m_n, l_n, o_n = softmax_parts(qr[...].reshape(n * M, HD), kv[:, :HD], kv[:, HD:], allowed > 0.5)
+    rb[:, :M] = o_n.reshape(n, M, HD)
+    rb[:, M:] = jnp.where(lane2 == 0, m_n, l_n).reshape(n, M, 128)
+    start_all(rb, rr, r_s, r_r)
+    rr[s] = rb[s]
+    wait_all(rb, rr, r_s, r_r)
+
+    o_n = rr[:, :M].reshape(n * M, HD)
+    ml = rr[:, M:].reshape(n * M, 128)
+    size = n * M
+    eye = lax.broadcasted_iota(jnp.int32, (size, size), 0) == lax.broadcasted_iota(jnp.int32, (size, size), 1)
+    m_row = jnp.sum(jnp.where(eye, ml[:, 0:1], 0.0), axis=0, keepdims=True)
+    l_row = jnp.sum(jnp.where(eye, ml[:, 1:2], 0.0), axis=0, keepdims=True)
+    id_row = jnp.sum(jnp.where(eye, ids[:, 0:1].astype(F32), 0.0), axis=0, keepdims=True)
+    mine = lax.broadcasted_iota(jnp.int32, (rows * heads, size), 0).astype(F32) == id_row
+    logit = jnp.where(mine, m_row, NEG_LARGE)
+    top = jnp.maximum(m_p, jnp.max(logit, axis=1, keepdims=True))
+    w = jnp.where(mine, jnp.exp(logit - top), 0.0)
+    scale = jnp.exp(m_p - top)
+    total = scale * l_p + jnp.sum(w * l_row, axis=1, keepdims=True)
+    acc[...] = (scale * om[...] + jnp.dot(w.astype(BF), o_n.astype(BF), preferred_element_type=F32)) / total
+    for h in range(heads):
+        att[s, :, h * HD:(h + 1) * HD] = acc[pl.ds(h, rows, stride=heads), :].astype(BF)
+
+    x, y, core = s // 8, (s // 2) % 4, s % 2
+    mate = (section_of(x, y, 1 - core), t)
+    xpeer = (section_of(1 - x, y, core), t)
+    ways = ((section_of(x, (y + 1) % 4, core), t), (section_of(x, (y + 3) % 4, core), t))
+
+    def ycopy(way, k, h):
+        xx = x if h == 0 else 1 - x
+        blk = section_of(xx, (y + (0 if k == 0 else (3 if way == 0 else 1))) % 4, core)
+        return remote(att.at[blk], att.at[blk], y_s.at[way, k, h], y_r.at[way, k, h], ways[way])
+
+    def ylast(way):
+        blk = section_of(way, (y + (3 if way == 0 else 1)) % 4, core)
+        return remote(att.at[blk], att.at[blk], y_s.at[way, 1, 0], y_r.at[way, 1, 0], ways[way])
+
+    def xcopy():
+        return remote(att.at[s], att.at[s], y_s.at[0, 1, 1], y_r.at[0, 1, 1], xpeer)
+
+    def give(i, blk):
+        c = remote(att.at[blk], att.at[blk], c_s.at[i], c_r.at[i], mate)
+        c.start()
+
+    xcopy().start()
+    for way in (0, 1):
+        ycopy(way, 0, 0).start()
+    give(0, s)
+    xcopy().wait_recv()
+    for way in (0, 1):
+        ycopy(way, 0, 1).start()
+    give(1, section_of(1 - x, y, core))
+    for way in (0, 1):
+        for h in (0, 1):
+            ycopy(way, 0, h).wait_recv()
+        ylast(way).start()
+        for h in (0, 1):
+            xx = x if h == 0 else 1 - x
+            give(2 + 2 * way + h, section_of(xx, (y + (3 if way == 0 else 1)) % 4, core))
+    for way in (0, 1):
+        ylast(way).wait_recv()
+        give(6 + way, section_of(way, (y + 2) % 4, core))
+    for i in range(8):
+        c = remote(att.at[s], att.at[s], c_s.at[i], c_r.at[i], mate)
+        c.wait_recv()
+        c.wait_send()
+    for way in (0, 1):
+        for h in (0, 1):
+            ycopy(way, 0, h).wait_send()
+        ylast(way).wait_send()
+    xcopy().wait_send()
+
+    @pl.loop(1, n)
+    def _(i):
+        exchange(tb, tr, t_s, t_r, i).wait_send()
+        exchange(qs, qr, q_s, q_r, i).wait_send()
+        exchange(rb, rr, r_s, r_r, i).wait_send()
+
+
+def attn_call(sec, row, q, tab, pool, arr):
+    rows = tab.shape[0]
+    n = 16
+    HD = q.shape[1]
+    heads = q.shape[0] // rows
+    M = CAP * heads
+    dma = pltpu.SemaphoreType.DMA
+    vm = pl.BlockSpec(memory_space=pltpu.VMEM)
+    hbm = pl.BlockSpec(memory_space=pl.ANY)
+    sm = pl.BlockSpec(memory_space=pltpu.SMEM)
+    return pl.pallas_call(
+        attn_kernel,
+        out_shape=jax.ShapeDtypeStruct((n, rows, heads * HD), BF),
+        in_specs=[sm, sm, vm, vm, hbm, hbm],
+        out_specs=vm,
+        scratch_shapes=[
+            pltpu.VMEM(pool.shape[1:], BF),
+            pltpu.VMEM(arr.shape[1:], BF),
+            pltpu.VMEM((n, M, 128), jnp.int32),
+            pltpu.VMEM((n, M, 128), jnp.int32),
+            pltpu.VMEM((n, M, HD), BF),
+            pltpu.VMEM((n, M, HD), BF),
+            pltpu.VMEM((n, 2 * M, HD), F32),
+            pltpu.VMEM((n, 2 * M, HD), F32),
+            pltpu.VMEM((rows * heads, HD), F32),
+            pltpu.VMEM((rows * heads, HD), F32),
+            dma((2,)), dma((n,)), dma((n,)), dma((n,)), dma((n,)), dma((n,)), dma((n,)),
+            dma((2, 2, 2)), dma((2, 2, 2)), dma((8,)), dma((8,)),
+        ],
+        compiler_params=pltpu.CompilerParams(
+            collective_id=3, has_side_effects=True, vmem_limit_bytes=VMEM_LIMIT),
+        name="attention",
+    )(sec, row, q, tab, pool, arr)
 
 
 def body(
@@ -516,51 +691,10 @@
     gate_weight,
     up_weight,
 ):
-    sections = lax.axis_size("section")
-    tensor_id = lax.axis_index("tensor")
-    kv_group = tensor_id // 2
-    row_count = queries.shape[0]
-    slot_count = kv_pool.shape[1]
-    block_len = kv_pool.shape[2]
-    features = kv_pool.shape[3]
-    own_pool = lax.dynamic_index_in_dim(kv_pool, kv_group, 0, keepdims=False).reshape(
-        slot_count * block_len, features
-    )
-    pool_allowed = cached_allowed(block_table, cached_lengths, slot_count, block_len)
-    own_new = lax.dynamic_index_in_dim(arrivals, kv_group, 0, keepdims=False)
-    sources = own_new.shape[0]
-    entry_ids = jnp.arange(sources)
-    same_dest = arrival_section[:, None] == arrival_section[None, :]
-    earlier = same_dest & (entry_ids[None, :] < entry_ids[:, None])
-    slot_rank = jnp.sum(earlier.astype(jnp.int32), axis=1)
-    target = arrival_section * CAP + slot_rank
-    placing = jnp.arange(sections * CAP)[:, None] == target[None, :]
-    send_blocks = jnp.dot(
-        placing.astype(jnp.bfloat16),
-        own_new.reshape(sources, block_len * features),
-        preferred_element_type=jnp.bfloat16,
-    )
-    send_blocks = send_blocks.reshape(sections, CAP, block_len, features)
-    send_rows = (jnp.sum(jnp.where(placing, arrival_row[None, :] + 1, 0), axis=1) - 1).reshape(
-        sections, CAP
-    )
-    got_blocks, got_rows = (
-        lax.all_to_all(send_blocks, "section", split_axis=0, concat_axis=0, tiled=True),
-        lax.all_to_all(send_rows, "section", split_axis=0, concat_axis=0, tiled=True),
-    )
-    arrived = got_blocks.reshape(sections * CAP * block_len, features)
-    owner_match = got_rows.reshape(sections * CAP)[None, :] == jnp.arange(row_count)[:, None]
-    new_allowed = jnp.broadcast_to(
-        owner_match[:, :, None], (row_count, sections * CAP, block_len)
-    ).reshape(row_count, sections * CAP * block_len)
-    highest, totals, summed = partial_softmax(
-        queries,
-        jnp.concatenate([own_pool, arrived], 0),
-        jnp.concatenate([pool_allowed, new_allowed], 1),
-    )
-    attention = (summed / totals[:, :, None]).astype(jnp.bfloat16).reshape(row_count, -1)
-    att = lax.all_gather(attention, "section", axis=0, tiled=True)
-    attn_proj, mg, sq = proj_call(att, out_weight, residual, norm_gain.reshape(1, -1))
+    rows, heads, head_dim = queries.shape
+    table = jnp.concatenate([block_table, cached_lengths[:, None]], axis=1)
+    att = attn_call(arrival_section, arrival_row, queries.reshape(rows * heads, head_dim), table, kv_pool, arrivals)
+    attn_proj, mg, sq = proj_call(att.reshape(-1, att.shape[2]), out_weight, residual, norm_gain.reshape(1, -1))
     hidden = ffn_call(mg.reshape(-1, mg.shape[2]), gate_weight, up_weight, sq)
     return (attn_proj, hidden)
 

time: 209 us -> 140 us (0.67)
  waiting for transfers between devices: 65.9 us -> 0 us
  Pallas kernels: 93.2 us -> 134 us
  between operations: 14.2 us -> 0.67 us
  starting transfers between devices: 12.3 us -> 0 us
  other arithmetic: 8.14 us -> 0.71 us
  matrix products: 6.11 us -> 0 us
  local copies, waits for them, and re-layouts: 8.67 us -> 4.45 us
    all_gather x1 -> x0, waiting for transfers between devices: 39.9 us -> none  [body(): att = lax.all_gather(attention, 'section', axis=0, tiled=True)]
    pallas_call x0 -> x1, Pallas kernels: none -> 39.2 us  [attn_call(): pl.pallas_call(attn_kernel, out_shape=jax.ShapeDtypeStruct((n, rows, head...]
    all_to_all x2 -> x0, waiting for transfers between devices: 26 us -> none  [the longest x1 25.3 us: body(): lax.all_to_all(send_blocks, 'section', split_axis=0, concat_axis=0, tiled...]
    all_to_all x2 -> x0, starting transfers between devices: 12.1 us -> none  [the longest x1 6.91 us: body(): lax.all_to_all(send_rows, 'section', split_axis=0, concat_axis=0, tiled=T...]
    dot_general x3 -> x0, matrix products: 6.11 us -> none  [the longest x1 2.68 us: partial_softmax(): jnp.einsum('rhk,kd->rhd', weights.astype(jnp.bfloat16), tokens[:, head_di...]
    sub x3 -> x0, other arithmetic: 4.99 us -> none  [the longest x1 4.32 us: partial_softmax(): weights = jnp.where(token_mask, jnp.exp(masked - highest[:, :, None]), 0.0)]
    pallas_call x1, Pallas kernels: 47.1 us -> 49.5 us  [proj_call(): pl.pallas_call(proj_kernel, out_shape=(jax.ShapeDtypeStruct((rows, width)...]
  transfers between devices with their start and end apart: 3 -> 0, of which waited for: 3 -> 0; matrix products, arithmetic and copies ran while one was open for 4% -> 0% of each run, Pallas kernels for 0% -> 0%
where the time goes in v2:
time: 140 us
  Pallas kernels  134 us (96%)
  local copies, waits for them, and re-layouts  4.45 us (3%)
    pallas_call x1, Pallas kernels, proj_call(): pl.pallas_call(proj_kernel, out_shape=(jax.ShapeDtypeStruct((rows, width)...  49.5 us
    pallas_call x1, Pallas kernels, ffn_call(): pl.pallas_call(ffn_kernel, out_shape=jax.ShapeDtypeStruct((rows, ffn), F3...  45.5 us
    pallas_call x1, Pallas kernels, attn_call(): pl.pallas_call(attn_kernel, out_shape=jax.ShapeDtypeStruct((n, rows, head...  39.2 us

profile of v2, /device:TPU:1, one launch (start us, length us, event | category | flops | bytes accessed | tf_op | source)
XLA Modules:
  0.0 139.9 jit_solution(10253873751990264958)
XLA Ops:
  0.6 1.3 reshape.18.gain
  1.9 0.7 pad_add_fusion
  2.6 0.7 copy.16.tab
  3.3 39.2 %attention.1 = bf16[16,64,1024]{2,1,0:T(8,128)(2,1)} custom-call(s32[8]{0:T(128)} %sec.1, s32[8]{0:T(128)} %row.1, bf16[512,128]{1,0:T(8,128)(2,1)} %bitcast.6, s32[64,5]{1,0:T(8,128)} %copy.16.tab, bf16[8,4,128,256]{3,2,1,0:T(8,128)(2,1)} %pool.1, bf16[8,8,128,256]{3,2,1,0:T(8,128)(2,1)} %arr.1), custom_call_target="tpu_custom_call" | custom-call | tf_op jit(solution)/shard_map/attention/pallas_call | solution.py:655
  42.5 49.5 %projection.1 = (f32[64,768]{1,0:T(8,128)}, bf16[16,64,768]{2,1,0:T(8,128)(2,1)}, f32[64,128]{1,0:T(8,128)}) custom-call(bf16[1024,1024]{1,0:T(8,128)(2,1)} %bitcast.4, bf16[1024,768]{1,0:T(8,128)(2,1)} %wo.1, bf16[64,768]{1,0:T(8,128)(2,1)} %res.1, bf16[1,768]{1,0:T(2,128)(2,1)} %reshape.18.gain), custom_call_target="tpu_custom_call" | custom-call | tf_op jit(solution)/shard_map/projection/pallas_call | solution.py:172
  92.0 0.0 copy-start
  92.0 45.5 %ffn.1 = f32[64,1664]{1,0:T(8,128)} custom-call(bf16[1024,768]{1,0:T(8,128)(2,1)} %bitcast.5, bf16[768,1664]{1,0:T(8,128)(2,1)} %gate.1, bf16[768,1664]{1,0:T(8,128)(2,1)} %up.1, f32[64,128]{1,0:T(8,128)} %get-tuple-element.7.sq), custom_call_target="tpu_custom_call" | custom-call | tf_op jit(solution)/shard_map/ffn/pallas_call | solution.py:442
  137.5 0.0 copy-done
  137.5 0.7 copy.19
  138.1 1.8 %copy.20 = f32[64,1664]{1,0:T(8,128)} copy(f32[64,1664]{1,0:T(8,128)} %ffn.1) | data formatting | bytes 851968
Async XLA Ops:
  92.0 45.5 %copy-start = (f32[64,768]{1,0:T(8,128)S(1)}, f32[64,768]{1,0:T(8,128)}, u32[]{:S(2)}) copy-start(f32[64,768]{1,0:T(8,128)} %get-tuple-element.10) | copy-start | bytes 589828

commit v3 on v0

v3 whole, which is shorter than its diff:
```python
import jax
import jax.numpy as jnp
from jax import lax
from jax.experimental import pallas as pl
from jax.experimental.pallas import tpu as pltpu
from jax.sharding import PartitionSpec as P

MESH = pl.DeviceIdType.MESH
CAP = 2
NEG_LARGE = -1e30
EPSILON = 1e-05
VMEM_LIMIT = 60 * 1024 * 1024
BF = jnp.bfloat16
F32 = jnp.float32
N = 16
CA = 512


def section_of(x, y, core):
    return x * 8 + y * 2 + core


def remote(src, dst, ssem, rsem, dev):
    return pltpu.make_async_remote_copy(
        src_ref=src, dst_ref=dst, send_sem=ssem, recv_sem=rsem,
        device_id=dev, device_id_type=MESH)


def signal(sem, dev):
    pl.semaphore_signal(sem, inc=1, device_id=dev, device_id_type=MESH)


def layer_kernel(sec, row, q, tab, lens, pool, arr, wo_in, res, gain, gate, up,
                 proj_out, hid,
                 kvp, kva, tb, tr, qs, qr, rb, rr, sp, om, acc, att, wo,
                 pz, rbuf, sbuf, xs, xr, mgf, wf,
                 pb, pa, bs, br, as_, ar, xas, xar, xbs, xbr, ps, pr, sq, sqr, fin,
                 l_sem, t_s, t_r, q_s, q_r, r_s, r_r, y_s, y_r, c_s, c_r,
                 rs_s, rs_r, px_s, px_r, ag_s, ag_r, gx_s, gx_r, mt_s, mt_r,
                 w_s, w_r, bss, brs, ass, ars, xass, xars, xbss, xbrs, pss, prs,
                 sqs, sqrs, dgs, dgr):
    s, t = lax.axis_index("section"), lax.axis_index("tensor")
    x, y, core = s // 8, (s // 2) % 4, s % 2
    xh, z = t // 8, t % 8
    diag = s == t
    off_diag = jnp.logical_not(diag)
    mate = (section_of(x, y, 1 - core), t)
    xpeer = (section_of(1 - x, y, core), t)
    hpeer = (s, (1 - xh) * 8 + z)

    def ydev(way):
        return (section_of(x, (y + 1 + 2 * way) % 4, core), t)

    def zdev(way):
        return (s, xh * 8 + (z + 1 + 6 * way) % 8)

    barrier = pltpu.get_barrier_semaphore()

    @pl.loop(1, N)
    def _(i):
        signal(barrier, ((s + i) % N, t))

    for dev in (zdev(0), zdev(1), hpeer):
        signal(barrier, dev)

    @pl.when(off_diag)
    def _():
        signal(barrier, (s, s))

    pool_copy = pltpu.make_async_copy(pool.at[t // 2], kvp, l_sem.at[0])
    arr_copy = pltpu.make_async_copy(arr.at[t // 2], kva, l_sem.at[1])
    wo_copy = pltpu.make_async_copy(wo_in, wo, l_sem.at[2])

    def w_own(c):
        return pltpu.make_async_copy(gate if c == 0 else up, wf.at[c], l_sem.at[3])

    def w_far(c):
        return remote(up if c == 0 else gate, wf.at[c], w_s, w_r, mate)

    pool_copy.start()
    arr_copy.start()
    wo_copy.start()

    HD = q.shape[1]
    rows = res.shape[0]
    heads = q.shape[0] // rows
    M = CAP * heads
    i2 = lax.broadcasted_iota(jnp.int32, (N * M, 128), 0)
    slot = i2 // heads
    head = i2 % heads
    secs = [sec[e] for e in range(sec.shape[0])]
    targets = []
    for e, d in enumerate(secs):
        rank = sum([(secs[p] == d).astype(jnp.int32) for p in range(e)], jnp.int32(0))
        targets.append(d * CAP + rank)
    ids = jnp.full((N * M, 128), -1, jnp.int32)
    for e, target in enumerate(targets):
        ids = jnp.where(slot == target, row[e] * heads + head, ids)
    tb[...] = ids.reshape(N, M, 128)

    def exchange(src, dst, ss, rs, i):
        d = (s + i) % N
        return remote(src.at[d], dst.at[s], ss.at[i], rs.at[i], (d, t))

    def start_all(src, dst, ss, rs):
        @pl.loop(1, N)
        def _(i):
            exchange(src, dst, ss, rs, i).start()

    def wait_all(src, dst, ss, rs):
        @pl.loop(1, N)
        def _(i):
            exchange(src, dst, ss, rs, i).wait_recv()

    @pl.when(diag)
    def _():
        pl.semaphore_wait(barrier, 2 * (N - 1) + 3)

    @pl.when(off_diag)
    def _():
        pl.semaphore_wait(barrier, N - 1 + 3)

    start_all(tb, tr, t_s, t_r)
    tr[s] = tb[s]
    for c in (0, 1):
        @pl.when(core == c)
        def _():
            w_own(c).start()
            w_far(c).start()

    blocks = kvp.shape[0]
    len_row = lens[...].reshape(1, rows)
    which = lax.broadcasted_iota(jnp.int32, (2 * blocks, rows), 0)
    limits = jnp.zeros((2 * blocks, rows), jnp.int32)
    for b in range(blocks):
        limit = jnp.zeros((1, rows), jnp.int32)
        for j in range(tab.shape[0]):
            limit = jnp.maximum(limit, jnp.where(tab[j:j + 1, :] == b, len_row - j * 128, 0))
        limits = jnp.where(which == b, limit // 2, jnp.where(which == blocks + b, limit % 2, limits))
    spread = (lax.broadcasted_iota(jnp.int32, (rows * heads, rows), 0) // heads
              == lax.broadcasted_iota(jnp.int32, (rows * heads, rows), 1)).astype(F32).astype(BF)
    limits = lax.dot_general(spread, limits.astype(F32).astype(BF), (((1,), (1,)), ((), ())),
                             preferred_element_type=F32)
    lane = lax.broadcasted_iota(jnp.int32, (rows * heads, 128), 1).astype(F32)
    ok = [lane < 2.0 * limits[:, b:b + 1] + limits[:, blocks + b:blocks + b + 1] for b in range(blocks)]
    pool_copy.wait()
    kv = kvp[...].reshape(-1, 2 * HD)
    scale_qk = HD ** -0.5

    def scores(a, k):
        return lax.dot_general(a, k, (((1,), (1,)), ((), ())), preferred_element_type=F32) * scale_qk

    okc = jnp.concatenate([o.astype(F32) for o in ok], axis=1) > 0.5
    sc = jnp.where(okc, scores(q[...], kv[:, :HD]), NEG_LARGE)
    m_p = jnp.max(sc, axis=1, keepdims=True)
    p = jnp.where(okc, jnp.exp(sc - m_p), 0.0)
    l_p = jnp.sum(p, axis=1, keepdims=True)
    om[...] = jnp.dot(p.astype(BF), kv[:, HD:], preferred_element_type=F32)

    wait_all(tb, tr, t_s, t_r)
    ids = tr[...].reshape(N * M, 128)
    lane2 = lax.broadcasted_iota(jnp.int32, (N * M, 128), 1)
    pick = jnp.concatenate([(ids == lane2 + 128 * c).astype(F32) for c in range(q.shape[0] // 128)], axis=1)
    qs[...] = jnp.dot(pick.astype(BF), q[...], preferred_element_type=F32).astype(BF).reshape(N, M, HD)
    start_all(qs, qr, q_s, q_r)
    qr[s] = qs[s]

    arr_copy.wait()
    kvn = kva[...].reshape(-1, 2 * HD)
    ok_n = jnp.concatenate([(slot == target).astype(F32) for target in targets], axis=1) > 0.5
    wait_all(qs, qr, q_s, q_r)
    sn = jnp.where(ok_n, scores(qr[...].reshape(N * M, HD), kvn[:, :HD]), NEG_LARGE)
    m_n = jnp.max(sn, axis=1, keepdims=True)
    pn = jnp.where(ok_n, jnp.exp(sn - m_n), 0.0)
    l_n = jnp.sum(pn, axis=1, keepdims=True)
    o_n = jnp.dot(pn.astype(BF), kvn[:, HD:], preferred_element_type=F32)
    rb[:, :M] = o_n.reshape(N, M, HD)
    rb[:, M:] = jnp.where(lane2 == 0, m_n, l_n).reshape(N, M, 128)
    start_all(rb, rr, r_s, r_r)
    rr[s] = rb[s]

    size = N * M
    eye = lax.broadcasted_iota(jnp.int32, (size, size), 0) == lax.broadcasted_iota(jnp.int32, (size, size), 1)
    id_row = jnp.sum(jnp.where(eye, ids[:, 0:1].astype(F32), 0.0), axis=0, keepdims=True)
    mine = lax.broadcasted_iota(jnp.int32, (rows * heads, size), 0).astype(F32) == id_row
    wait_all(rb, rr, r_s, r_r)
    o_n = rr[:, :M].reshape(size, HD)
    ml = rr[:, M:].reshape(size, 128)
    m_row = jnp.sum(jnp.where(eye, ml[:, 0:1], 0.0), axis=0, keepdims=True)
    l_row = jnp.sum(jnp.where(eye, ml[:, 1:2], 0.0), axis=0, keepdims=True)
    logit = jnp.where(mine, m_row, NEG_LARGE)
    top = jnp.maximum(m_p, jnp.max(logit, axis=1, keepdims=True))
    w = jnp.where(mine, jnp.exp(logit - top), 0.0)
    scale = jnp.exp(m_p - top)
    total = scale * l_p + jnp.sum(w * l_row, axis=1, keepdims=True)
    acc[...] = (scale * om[...] + jnp.dot(w.astype(BF), o_n.astype(BF), preferred_element_type=F32)) / total
    for h in range(heads):
        att[s, :, h * HD:(h + 1) * HD] = acc[pl.ds(h, rows, stride=heads), :].astype(BF)

    def ycopy(way, h):
        xx = x if h == 0 else 1 - x
        src = section_of(xx, y, core)
        return remote(att.at[src], att.at[src], y_s.at[way, 0, h], y_r.at[way, 0, h], ydev(way))

    def ylast(way):
        blk = section_of(way, (y + 3 - 2 * way) % 4, core)
        return remote(att.at[blk], att.at[blk], y_s.at[way, 1, 0], y_r.at[way, 1, 0], ydev(way))

    def xcopy():
        return remote(att.at[s], att.at[s], y_s.at[0, 1, 1], y_r.at[0, 1, 1], xpeer)

    def give(i, blk):
        remote(att.at[blk], att.at[blk], c_s.at[i], c_r.at[i], mate).start()

    xcopy().start()
    for way in (0, 1):
        ycopy(way, 0).start()
    give(0, s)
    xcopy().wait_recv()
    for way in (0, 1):
        ycopy(way, 1).start()
    give(1, section_of(1 - x, y, core))
    for way in (0, 1):
        for h in (0, 1):
            ycopy(way, h).wait_recv()
        ylast(way).start()
        for h in (0, 1):
            give(2 + 2 * way + h, section_of(x if h == 0 else 1 - x, (y + 3 - 2 * way) % 4, core))
    for way in (0, 1):
        ylast(way).wait_recv()
        give(6 + way, section_of(way, (y + 2) % 4, core))
    wo_copy.wait()
    for i in range(8):
        remote(att.at[s], att.at[s], c_s.at[i], c_r.at[i], mate).wait_recv()

    def project(slot_, off):
        zz = (z + off) % 8
        a = jnp.concatenate([att[zz], att[8 + zz]], 0)
        v = jnp.dot(a, wo[...], preferred_element_type=F32)
        pz[slot_, 0] = v[:rows]
        pz[slot_, 1] = v[rows:]

    def off_of(slot_):
        k = (slot_ + 1) // 2
        return jnp.where(slot_ % 2 == 1, 4 - k, 4 + k) % 8

    def rs(way, k, h):
        return remote(sbuf.at[way, k, h], rbuf.at[way, k, h], rs_s.at[way, k, h], rs_r.at[way, k, h], zdev(way))

    def rs_send(way, k, h, add):
        v = pz[0 if k == 0 else 2 * k - 1 + way, h]
        if add:
            rs(way, k - 1, h).wait_recv()
            v = v + rbuf[way, k - 1, h].astype(F32)
        sbuf[way, k, h] = v.astype(BF)
        rs(way, k, h).start()

    halves = (1 - xh, xh)
    project(0, 4)
    for h in halves:
        rs_send(h, 0, h, False)

    @pl.loop(1, 3)
    def _(i):
        project(i, off_of(i))

    for h in halves:
        rs_send(1 - h, 1, h, False)

    @pl.loop(3, 8)
    def _(i):
        project(i, off_of(i))

    for k in (1, 2, 3):
        for h in halves:
            rs_send(h, k, h, True)
            if k > 1:
                rs_send(1 - h, k, h, True)

    def rs_total(h):
        for way in (0, 1):
            rs(way, 3, h).wait_recv()
        return pz[7, h] + rbuf[0, 3, h].astype(F32) + rbuf[1, 3, h].astype(F32)

    def pair_copy():
        return remote(xs, xr, px_s, px_r, hpeer)

    xs[...] = rs_total(1 - xh).astype(BF)
    pair_copy().start()
    part_own = rs_total(xh)
    pair_copy().wait_recv()
    proj = part_own + xr[...].astype(F32)
    mixed = proj + res[...].astype(F32)
    mgf[core, t] = (mixed * gain[...].reshape(1, -1).astype(F32)).astype(BF)

    def agx():
        return remote(mgf.at[core, t], mgf.at[core, t], gx_s, gx_r, hpeer)

    def blk_of(way, k, r):
        return (xh if r == 0 else 1 - xh) * 8 + (z + 8 + (2 * way - 1) * k) % 8

    def ag(way, k, r):
        ref = mgf.at[core, blk_of(way, k, r)]
        return remote(ref, ref, ag_s.at[way, k, r], ag_r.at[way, k, r], zdev(way))

    def main(r):
        return xh if r == 0 else 1 - xh

    def hand(r, i, blk):
        ref = mgf.at[core, blk]
        remote(ref, ref, mt_s.at[r, i], mt_r.at[r, i], mate).start()

    def hand_wait(r):
        for i in range(8):
            ref = mgf.at[core, t]
            remote(ref, ref, mt_s.at[r, i], mt_r.at[r, i], mate).wait_recv()

    def ag_step(k, r):
        for way in (0, 1):
            ag(way, k - 1, r).wait_recv()
            if k < 3:
                ag(way, k, r).start()
        if k == 3:
            ag(main(r), 3, r).start()
        for way in (0, 1):
            hand(r, 2 * (k - 1) + 1 + way, blk_of(way, k, r))

    def ag_end(r):
        ag(main(r), 3, r).wait_recv()
        hand(r, 7, blk_of(0, 4, r))

    for way in (0, 1):
        ag(way, 0, 0).start()
    agx().start()
    hand(0, 0, t)
    proj_out[...] = proj
    sq[...] = jnp.sum(mixed * mixed, axis=1, keepdims=True) + jnp.zeros(sq.shape, F32)

    def sq_copy(i):
        return remote(sq, sqr.at[i], sqs, sqrs.at[i], (t, t))

    def dg_copy(i):
        return remote(fin, fin, dgs.at[i], dgr, (s, (t + i) % N))

    @pl.when(off_diag)
    def _():
        sq_copy((s - t + N) % N).start()

    ag_step(1, 0)
    agx().wait_recv()
    for way in (0, 1):
        ag(way, 0, 1).start()
    hand(1, 0, (1 - xh) * 8 + z)
    ag_step(2, 0)
    ag_step(1, 1)
    ag_step(3, 0)
    ag_end(0)

    R = 2 * rows
    FFN = gate.shape[1]
    CB = FFN - CA
    H = CA // 2
    for c in (0, 1):
        @pl.when(core == c)
        def _():
            w_own(c).wait()
            w_far(c).wait_recv()

    def yoff(k):
        return (y + jnp.where(k == 0, 2, jnp.where(k == 1, 1, jnp.where(k == 2, 3, 0)))) % 4

    def ffn_part(hf, pos, hx):
        k = (0, 2 - hx, 1 + hx, 3)[pos]
        b = hx * 8 + 2 * yoff(k)
        a0 = mgf[0, pl.ds(b, 2)].reshape(R, -1)
        a1 = mgf[1, pl.ds(b, 2)].reshape(R, -1)

        def cols(c0, c1):
            return (jnp.dot(a0, wf[0, :, c0:c1], preferred_element_type=F32)
                    + jnp.dot(a1, wf[1, :, c0:c1], preferred_element_type=F32))

        pb[hf, pos] = cols(CA, FFN)
        pa[hf, pos] = cols(0, CA)

        @pl.when(hx != x)
        def _():
            xas[pos] = pa[hf, pos].astype(BF)
            xacopy(pos).start()

    def bcopy(way, m):
        return remote(bs.at[way, m], br.at[way, m], bss.at[way, m], brs.at[way, m], ydev(way))

    def acopy(way, m):
        return remote(as_.at[way, m], ar.at[way, m], ass.at[way, m], ars.at[way, m], ydev(way))

    def xacopy(k):
        return remote(xas.at[k], xar.at[k], xass.at[k], xars.at[k], xpeer)

    def xbcopy():
        return remote(xbs, xbr, xbss, xbrs, xpeer)

    def ffn_half(hf, hx, between):
        hand_wait(hf)
        ffn_part(hf, 0, hx)
        bs[hx, 0] = pb[hf, 0].astype(BF)
        bcopy(hx, 0).start()
        between(0)
        ffn_part(hf, 1, hx)
        bs[1 - hx, 1] = pb[hf, 1].astype(BF)
        bcopy(1 - hx, 1).start()
        between(1)
        ffn_part(hf, 2, hx)
        between(2)
        bcopy(hx, 0).wait_recv()
        bs[hx, 2] = (pb[hf, 2] + br[hx, 0].astype(F32)).astype(BF)
        bcopy(hx, 2).start()
        ffn_part(hf, 3, hx)

    def between(i):
        if i == 0:
            ag_step(2, 1)
        elif i == 1:
            ag_step(3, 1)
        else:
            ag_end(1)

    ffn_half(0, xh, between)
    ffn_half(1, 1 - xh, lambda i: None)

    ho = jnp.where(x == xh, 0, 1)

    def a_sum(pos):
        xacopy(pos).wait_recv()
        pa[ho, pos] = pa[ho, pos] + xar[pos].astype(F32)

    def a_pos(way):
        return jnp.where(way == x, 2, 1)

    a_sum(0)
    for way in (0, 1):
        as_[way, 0] = pa[ho, 0, :, way * H:(way + 1) * H].astype(BF)
        acopy(way, 0).start()
    a_sum(1)
    a_sum(2)
    for way in (0, 1):
        as_[way, 1] = pa[ho, a_pos(way), :, (1 - way) * H:(2 - way) * H].astype(BF)
        acopy(way, 1).start()

    for way in (0, 1):
        bcopy(way, 1).wait_recv()
        bcopy(way, 2).wait_recv()
    for hf, hx in ((0, xh), (1, 1 - xh)):
        pb[hf, 3] = pb[hf, 3] + br[hx, 2].astype(F32) + br[1 - hx, 1].astype(F32)
    xbs[...] = pb[1 - ho, 3].astype(BF)
    xbcopy().start()

    for way in (0, 1):
        acopy(way, 0).wait_recv()
        as_[way, 2] = (pa[ho, a_pos(way), :, way * H:(way + 1) * H] + ar[way, 0].astype(F32)).astype(BF)
        acopy(way, 2).start()

    @pl.when(diag)
    def _():
        acc_sq = sq[...]
        for i in range(1, N):
            sq_copy(i).wait_recv()
            acc_sq = acc_sq + sqr[i]
        fin[...] = acc_sq
        for i in range(1, N):
            dg_copy(i).start()

    a_sum(3)
    for way in (0, 1):
        acopy(way, 1).wait_recv()
        acopy(way, 2).wait_recv()
    for h in (0, 1):
        pa[ho, 3, :, h * H:(h + 1) * H] = (pa[ho, 3, :, h * H:(h + 1) * H]
                                           + ar[h, 2].astype(F32) + ar[1 - h, 1].astype(F32))

    give_rows = pl.multiple_of((1 - core) * rows, rows)
    keep_rows = pl.multiple_of(core * rows, rows)

    def pcopy(i):
        c = (slice(0, CA), slice(CA, FFN))[i]
        return remote(ps.at[:, c], pr.at[:, c], pss.at[i], prs.at[i], mate)

    ps[:, :CA] = pa[ho, 3, pl.ds(give_rows, rows), :]
    pcopy(0).start()
    xbcopy().wait_recv()
    pb[ho, 3] = pb[ho, 3] + xbr[...].astype(F32)
    ps[:, CA:] = pb[ho, 3, pl.ds(give_rows, rows), :]
    pcopy(1).start()

    @pl.when(off_diag)
    def _():
        dg_copy(1).wait_recv()

    inv = lax.rsqrt(fin[:, :1] / (gate.shape[0] * N) + EPSILON)

    def finish(i, own, c0, c1):
        pcopy(i).wait_recv()
        other = pr[:, c0:c1] * inv
        own = own * inv
        g = jnp.where(core == 0, own, other)
        u = jnp.where(core == 0, other, own)
        hid[:, c0:c1] = g / (1.0 + jnp.exp(-g)) * u

    finish(0, pa[ho, 3, pl.ds(keep_rows, rows), :], 0, CA)
    finish(1, pb[ho, 3, pl.ds(keep_rows, rows), :], CA, FFN)

    @pl.loop(1, N)
    def _(i):
        exchange(tb, tr, t_s, t_r, i).wait_send()
        exchange(qs, qr, q_s, q_r, i).wait_send()
        exchange(rb, rr, r_s, r_r, i).wait_send()

    for i in range(8):
        remote(att.at[s], att.at[s], c_s.at[i], c_r.at[i], mate).wait_send()
        for r in (0, 1):
            ref = mgf.at[core, t]
            remote(ref, ref, mt_s.at[r, i], mt_r.at[r, i], mate).wait_send()
    xcopy().wait_send()
    pair_copy().wait_send()
    agx().wait_send()
    xbcopy().wait_send()
    for way in (0, 1):
        for h in (0, 1):
            ycopy(way, h).wait_send()
            rs(way, 1, h).wait_send()
            rs(way, 2, h).wait_send()
            rs(way, 3, h).wait_send()
            for k in range(3):
                ag(way, k, h).wait_send()
        ylast(way).wait_send()
        rs(way, 0, way).wait_send()
        ag(main(way), 3, way).wait_send()
        for m in range(3):
            bcopy(way, m).wait_send()
            acopy(way, m).wait_send()
    for k in range(4):
        xacopy(k).wait_send()
    for i in (0, 1):
        pcopy(i).wait_send()
    for c in (0, 1):
        @pl.when(core == c)
        def _():
            w_far(c).wait_send()

    @pl.when(diag)
    def _():
        for i in range(1, N):
            dg_copy(i).wait_send()

    @pl.when(off_diag)
    def _():
        sq_copy((s - t + N) % N).wait_send()


def body(
    queries,
    kv_pool,
    block_table,
    cached_lengths,
    arrivals,
    arrival_section,
    arrival_row,
    out_weight,
    residual,
    norm_gain,
    gate_weight,
    up_weight,
):
    rows, heads, hd = queries.shape
    width, ffn = gate_weight.shape
    m = CAP * heads
    cb = ffn - CA
    vm = pl.BlockSpec(memory_space=pltpu.VMEM)
    hbm = pl.BlockSpec(memory_space=pl.ANY)
    sm = pl.BlockSpec(memory_space=pltpu.SMEM)
    dma = pltpu.SemaphoreType.DMA

    def v(*shape, dtype=BF):
        return pltpu.VMEM(shape, dtype)

    scratch = [
        v(*kv_pool.shape[1:]), v(*arrivals.shape[1:]),
        v(N, m, 128, dtype=jnp.int32), v(N, m, 128, dtype=jnp.int32),
        v(N, m, hd), v(N, m, hd),
        v(N, 2 * m, hd, dtype=F32), v(N, 2 * m, hd, dtype=F32),
        v(rows * heads, kv_pool.shape[1] * kv_pool.shape[2], dtype=F32),
        v(rows * heads, hd, dtype=F32), v(rows * heads, hd, dtype=F32),
        v(N, rows, heads * hd), v(*out_weight.shape),
        v(8, 2, rows, width, dtype=F32), v(2, 4, 2, rows, width), v(2, 4, 2, rows, width),
        v(rows, width), v(rows, width), v(2, N, rows, width), v(2, width, ffn),
        v(2, 4, 2 * rows, cb, dtype=F32), v(2, 4, 2 * rows, CA, dtype=F32),
        v(2, 3, 2 * rows, cb), v(2, 3, 2 * rows, cb),
        v(2, 3, 2 * rows, CA // 2), v(2, 3, 2 * rows, CA // 2),
        v(4, 2 * rows, CA), v(4, 2 * rows, CA),
        v(2 * rows, cb), v(2 * rows, cb),
        v(rows, ffn, dtype=F32), v(rows, ffn, dtype=F32),
        v(rows, 128, dtype=F32), v(N, rows, 128, dtype=F32), v(rows, 128, dtype=F32),
        dma((4,)), dma((N,)), dma((N,)), dma((N,)), dma((N,)), dma((N,)), dma((N,)),
        dma((2, 2, 2)), dma((2, 2, 2)), dma((8,)), dma((8,)),
        dma((2, 4, 2)), dma((2, 4, 2)), dma, dma, dma((2, 4, 2)), dma((2, 4, 2)), dma, dma,
        dma((2, 8)), dma((2, 8)),
        dma, dma, dma((2, 3)), dma((2, 3)), dma((2, 3)), dma((2, 3)),
        dma((4,)), dma((4,)), dma, dma, dma((2,)), dma((2,)),
        dma, dma((N,)), dma((N,)), dma,
    ]
    return pl.pallas_call(
        layer_kernel,
        out_shape=(jax.ShapeDtypeStruct(residual.shape, F32), jax.ShapeDtypeStruct((rows, ffn), F32)),
        in_specs=[sm, sm, vm, vm, vm, hbm, hbm, hbm, vm, vm, hbm, hbm],
        out_specs=(vm, vm),
        scratch_shapes=scratch,
        compiler_params=pltpu.CompilerParams(
            collective_id=1, has_side_effects=True, vmem_limit_bytes=VMEM_LIMIT),
        name="layer",
    )(arrival_section, arrival_row, queries.reshape(rows * heads, hd), block_table.T, cached_lengths,
      kv_pool, arrivals, out_weight, residual, norm_gain, gate_weight, up_weight)


def solution(mesh):
    placed = (
        P("section", "tensor", None),
        P(None, "section", None, None),
        P("section", None),
        P("section"),
        P(None, "section", None, None),
        P("section"),
        P("section"),
        P("tensor", "section"),
        P("tensor", "section"),
        P("section"),
        P("section", "tensor"),
        P("section", "tensor"),
    )
    return jax.shard_map(
        body,
        mesh=mesh,
        in_specs=placed,
        out_specs=(P("tensor", "section"), P("section", "tensor")),
        check_vma=False,
    )
```

time: 534 us -> 130 us (0.24)
  waiting for transfers between devices: 430 us -> 0 us
  Pallas kernels: 0 us -> 124 us
  blocking collectives: 31.1 us -> 0 us
  matrix products: 19.2 us -> 0 us
  other arithmetic: 18.1 us -> 0 us
  between operations: 14 us -> 0.64 us
  starting transfers between devices: 12.4 us -> 0 us
    reduce_scatter x2 -> x0, waiting for transfers between devices: 290 us -> none  [the longest x1 205 us: body(): lax.psum_scatter(partial_proj, 'tensor', scatter_dimension=0, tiled=True)]
    pallas_call x0 -> x1, Pallas kernels: none -> 124 us  [body(): pl.pallas_call(layer_kernel, out_shape=(jax.ShapeDtypeStruct(residual.sha...]
    all_gather x2 -> x0, waiting for transfers between devices: 115 us -> none  [the longest x1 74.3 us: body(): segment = lax.all_gather(normed, 'tensor', axis=0, tiled=True)]
    psum x1 -> x0, blocking collectives: 31.1 us -> none  [body(): squares = lax.psum(jnp.sum(combined * combined, axis=1), 'section')]
    all_to_all x2 -> x0, waiting for transfers between devices: 25.3 us -> none  [the longest x1 24.6 us: body(): lax.all_to_all(send_blocks, 'section', split_axis=0, concat_axis=0, tiled...]
    dot_general x6 -> x0, matrix products: 19.2 us -> none  [the longest x1 5.48 us: body(): jnp.dot(lax.all_gather(attention, 'section', axis=0, tiled=True), out_wei...]
    all_to_all x2 -> x0, starting transfers between devices: 12.1 us -> none  [the longest x1 6.91 us: body(): lax.all_to_all(send_rows, 'section', split_axis=0, concat_axis=0, tiled=T...]
  transfers between devices with their start and end apart: 6 -> 0, of which waited for: 6 -> 0; matrix products, arithmetic and copies ran while one was open for 2% -> 0% of each run, Pallas kernels for 0% -> 0%
where the time goes in v3:
time: 130 us; the launch traced here: 128 us
  Pallas kernels  124 us (95%)
  local copies, waits for them, and re-layouts  3.41 us (3%)
    pallas_call x1, Pallas kernels, body(): pl.pallas_call(layer_kernel, out_shape=(jax.ShapeDtypeStruct(residual.sha...  124 us
    unnamed x2, local copies, waits for them, and re-layouts  3.41 us

profile of v3, /device:TPU:1, one launch (start us, length us, event | category | flops | bytes accessed | tf_op | source)
XLA Modules:
  0.0 127.7 jit_solution(16197061587583905822)
XLA Ops:
  0.6 123.7 %layer.1 = (f32[64,768]{1,0:T(8,128)}, f32[64,1664]{1,0:T(8,128)}) custom-call(s32[8]{0:T(128)} %sec.1, s32[8]{0:T(128)} %row.1, bf16[512,128]{1,0:T(8,128)(2,1)} %bitcast.2, s32[4,64]{1,0:T(4,128)} %bitcast.3, s32[64]{0:T(128)} %lens.1, bf16[8,4,128,256]{3,2,1,0:T(8,128)(2,1)} %pool.1, bf16[8,8,128,256]{3,2,1,0:T(8,128)(2,1)} %arr.1, ...), custom_call_target="tpu_custom_call" | custom-call | tf_op jit(solution)/shard_map/layer/pallas_call | solution.py:610
  124.3 1.6 %copy.16 = f32[64,768]{1,0:T(8,128)} copy(f32[64,768]{1,0:T(8,128)} %get-tuple-element.4) | data formatting | bytes 393216
  125.9 1.8 %copy.17 = f32[64,1664]{1,0:T(8,128)} copy(f32[64,1664]{1,0:T(8,128)} %get-tuple-element.5) | data formatting | bytes 851968

commit v4 on v3

v4 whole, which is shorter than its diff:
```python
import jax
import jax.numpy as jnp
from jax import lax
from jax.experimental import pallas as pl
from jax.experimental.pallas import tpu as pltpu
from jax.sharding import PartitionSpec as P

MESH = pl.DeviceIdType.MESH
CAP = 2
NEG_LARGE = -1e30
EPSILON = 1e-05
VMEM_LIMIT = 60 * 1024 * 1024
BF = jnp.bfloat16
F32 = jnp.float32
N = 16
CA = 512
PZ = (4, 2)
PP = 2
PA = 2
PB = 4
PX = 2


def section_of(x, y, core):
    return x * 8 + y * 2 + core


def remote(src, dst, ssem, rsem, dev):
    return pltpu.make_async_remote_copy(
        src_ref=src, dst_ref=dst, send_sem=ssem, recv_sem=rsem,
        device_id=dev, device_id_type=MESH)


def signal(sem, dev):
    pl.semaphore_signal(sem, inc=1, device_id=dev, device_id_type=MESH)


def layer_kernel(sec, row, q, tab, lens, pool, arr, wo_in, res, gain, gate, up,
                 proj_out, hid,
                 kvp, kva, tb, tr, qs, qr, eb, ef, acc, att, wo, dh, dl, dwh, dwl, idr,
                 pz, rbuf, sbuf, xs, xr, resx, mgf, wf,
                 pb, pa, bs, br, as_, ar, xas, xar, xbs, xbr, ps, pr, sq, sqr, fin,
                 l_sem, t_s, t_r, q_s, q_r, e_s, e_r, eg_s, eg_r, y_s, y_r, c_s, c_r,
                 rs_s, rs_r, px_s, px_r, ag_s, ag_r, rx_s, rx_r, mt_s, mt_r,
                 w_s, w_r, bss, brs, ass, ars, xass, xars, xbss, xbrs, pss, prs,
                 sqs, sqrs, dgs, dgr):
    s, t = lax.axis_index("section"), lax.axis_index("tensor")
    x, y, core = s // 8, (s // 2) % 4, s % 2
    xh, z = t // 8, t % 8
    diag = s == t
    off_diag = jnp.logical_not(diag)
    mate = (section_of(x, y, 1 - core), t)
    xpeer = (section_of(1 - x, y, core), t)
    hpeer = (s, (1 - xh) * 8 + z)

    def ydev(way):
        return (section_of(x, (y + 1 + 2 * way) % 4, core), t)

    def zdev(way):
        return (s, xh * 8 + (z + 1 + 6 * way) % 8)

    barrier = pltpu.get_barrier_semaphore()

    @pl.loop(1, N)
    def _(i):
        signal(barrier, ((s + i) % N, t))

    for dev in (zdev(0), zdev(1), hpeer):
        signal(barrier, dev)

    @pl.when(off_diag)
    def _():
        signal(barrier, (s, s))

    pool_copy = pltpu.make_async_copy(pool.at[t // 2], kvp, l_sem.at[0])
    arr_copy = pltpu.make_async_copy(arr.at[t // 2], kva, l_sem.at[1])
    wo_copy = pltpu.make_async_copy(wo_in, wo, l_sem.at[2])

    def w_own(c):
        return pltpu.make_async_copy(gate if c == 0 else up, wf.at[c], l_sem.at[3])

    def w_far(c):
        return remote(up if c == 0 else gate, wf.at[c], w_s, w_r, mate)

    pool_copy.start()
    arr_copy.start()
    wo_copy.start()

    HD = q.shape[1]
    rows = res.shape[0]
    heads = q.shape[0] // rows
    M = CAP * heads
    i2 = lax.broadcasted_iota(jnp.int32, (N * M, 128), 0)
    slot = i2 // heads
    head = i2 % heads
    secs = [sec[e] for e in range(sec.shape[0])]
    targets = []
    for e, d in enumerate(secs):
        rank = sum([(secs[p] == d).astype(jnp.int32) for p in range(e)], jnp.int32(0))
        targets.append(d * CAP + rank)
    ids = jnp.full((N * M, 128), -1, jnp.int32)
    for e, target in enumerate(targets):
        ids = jnp.where(slot == target, row[e], ids)
    tb[...] = ids.astype(F32).astype(BF).reshape(N, M, 128)

    def exchange(src, dst, ss, rs, i):
        d = (s + i) % N
        return remote(src.at[d], dst.at[s], ss.at[i], rs.at[i], (d, t))

    def start_all(src, dst, ss, rs):
        @pl.loop(1, N)
        def _(i):
            exchange(src, dst, ss, rs, i).start()

    def wait_all(src, dst, ss, rs):
        @pl.loop(1, N)
        def _(i):
            exchange(src, dst, ss, rs, i).wait_recv()

    @pl.when(diag)
    def _():
        pl.semaphore_wait(barrier, 2 * (N - 1) + 3)

    @pl.when(off_diag)
    def _():
        pl.semaphore_wait(barrier, N - 1 + 3)

    start_all(tb, tr, t_s, t_r)
    tr[s] = tb[s]

    def res_copy():
        return remote(res, resx, rx_s, rx_r, hpeer)

    res_copy().start()
    for c in (0, 1):
        @pl.when(core == c)
        def _():
            w_own(c).start()
            w_far(c).start()

    blocks = kvp.shape[0]
    len_row = lens[...].reshape(1, rows)
    which = lax.broadcasted_iota(jnp.int32, (2 * blocks, rows), 0)
    limits = jnp.zeros((2 * blocks, rows), jnp.int32)
    for b in range(blocks):
        limit = jnp.zeros((1, rows), jnp.int32)
        for j in range(tab.shape[0]):
            limit = jnp.maximum(limit, jnp.where(tab[j:j + 1, :] == b, len_row - j * 128, 0))
        limits = jnp.where(which == b, limit // 2, jnp.where(which == blocks + b, limit % 2, limits))
    def spread_of(shape, axis):
        return (lax.broadcasted_iota(jnp.int32, shape, axis) // heads
                == lax.broadcasted_iota(jnp.int32, shape, 1 - axis)).astype(F32).astype(BF)

    spread = spread_of((rows * heads, rows), 0)
    limits = lax.dot_general(spread, limits.astype(F32).astype(BF), (((1,), (1,)), ((), ())),
                             preferred_element_type=F32)
    lane = lax.broadcasted_iota(jnp.int32, (rows * heads, 128), 1).astype(F32)
    ok = [lane < 2.0 * limits[:, b:b + 1] + limits[:, blocks + b:blocks + b + 1] for b in range(blocks)]
    pool_copy.wait()
    kv = kvp[...].reshape(-1, 2 * HD)
    scale_qk = HD ** -0.5

    def scores(a, k):
        return lax.dot_general(a, k, (((1,), (1,)), ((), ())), preferred_element_type=F32) * scale_qk

    okc = jnp.concatenate([o.astype(F32) for o in ok], axis=1) > 0.5
    sc = jnp.where(okc, scores(q[...], kv[:, :HD]), NEG_LARGE)
    m_p = jnp.max(sc, axis=1, keepdims=True)
    p = jnp.where(okc, jnp.exp(sc - m_p), 0.0)
    l_p = jnp.sum(p, axis=1, keepdims=True)
    acc[...] = jnp.dot(p.astype(BF), kv[:, HD:], preferred_element_type=F32) / l_p
    for h in range(heads):
        att[s, :, h * HD:(h + 1) * HD] = acc[pl.ds(h, rows, stride=heads), :].astype(BF)

    def terms(v):
        hi = v.astype(BF).astype(F32)
        mid = (v - hi).astype(BF).astype(F32)
        return hi, mid, v - hi - mid

    lane_i = lax.broadcasted_iota(jnp.int32, (rows * heads, 128), 1)
    row_i = lax.broadcasted_iota(jnp.int32, (rows * heads, 128), 0)
    stats = jnp.zeros((rows * heads, 128), F32)
    for i, term in enumerate(terms(m_p) + terms(l_p)):
        stats = jnp.where(lane_i // heads == i, term, stats)
    stats = jnp.where(lane_i % heads == row_i % heads, stats, 0.0)
    att[s, :, heads * HD:] = jnp.dot(spread_of((rows, rows * heads), 1), stats.astype(BF),
                                     preferred_element_type=F32).astype(BF)

    def rows_of(ref, blk, pc, pieces):
        step = rows // pieces
        return ref.at[blk, pl.ds(pc * step, step)]

    def ycopy(way, h, pc):
        ref = rows_of(att, section_of(x if h == 0 else 1 - x, y, core), pc, PA)
        return remote(ref, ref, y_s.at[way, h, pc], y_r.at[way, h, pc], ydev(way))

    def ylast(way, pc):
        ref = rows_of(att, section_of(way, (y + 3 - 2 * way) % 4, core), pc, PA)
        return remote(ref, ref, y_s.at[way, 2, pc], y_r.at[way, 2, pc], ydev(way))

    def xcopy(pc):
        ref = rows_of(att, s, pc, PA)
        return remote(ref, ref, y_s.at[0, 3, pc], y_r.at[0, 3, pc], xpeer)

    def give(i, blk):
        remote(att.at[blk], att.at[blk], c_s.at[i], c_r.at[i], mate).start()

    for pc in range(PA):
        xcopy(pc).start()
        for way in (0, 1):
            ycopy(way, 0, pc).start()
    give(0, s)

    wait_all(tb, tr, t_s, t_r)
    asked = tr[...].reshape(N * M, 128).astype(F32)
    ids = jnp.where(asked < 0.0, -1.0, asked * heads + head.astype(F32))
    lane2 = lax.broadcasted_iota(jnp.int32, (N * M, 128), 1)
    pick = jnp.concatenate([(ids == (lane2 + 128 * c).astype(F32)).astype(F32) for c in range(q.shape[0] // 128)], axis=1)
    qs[...] = jnp.dot(pick.astype(BF), q[...], preferred_element_type=F32).astype(BF).reshape(N, M, HD)
    start_all(qs, qr, q_s, q_r)
    qr[s] = qs[s]

    for pc in range(PA):
        xcopy(pc).wait_recv()
        for way in (0, 1):
            ycopy(way, 1, pc).start()
        ycopy(x, 0, pc).wait_recv()
        ylast(x, pc).start()
    give(1, section_of(1 - x, y, core))

    E = len(targets)
    HE = heads * E
    arr_copy.wait()
    kvn = kva[...].reshape(-1, 2 * HD)
    slot_of = lax.broadcasted_iota(jnp.int32, (HE, N * M), 0)
    want = jnp.zeros((HE, N * M), jnp.int32)
    for e, target in enumerate(targets):
        want = jnp.where(slot_of % E == e, target * heads + slot_of // E, want)
    sel = (want == lax.broadcasted_iota(jnp.int32, (HE, N * M), 1)).astype(F32).astype(BF)
    ok_n = (lax.broadcasted_iota(jnp.int32, (HE, E * 128), 1) // 128
            == lax.broadcasted_iota(jnp.int32, (HE, E * 128), 0) % E)
    lane_e = lax.broadcasted_iota(jnp.int32, (HE, 128), 1)
    entry = lax.broadcasted_iota(jnp.int32, (HE, 128), 0) % E
    place = jnp.zeros((HE, 128), jnp.int32)
    for e in range(E):
        place = jnp.where(entry == e, jnp.where(lane_e == 6, secs[e], row[e]), place)
    wait_all(qs, qr, q_s, q_r)
    qn = jnp.dot(sel, qr[...].reshape(N * M, HD), preferred_element_type=F32).astype(BF)
    sn = jnp.where(ok_n, scores(qn, kvn[:, :HD]), NEG_LARGE)
    m_n = jnp.max(sn, axis=1, keepdims=True)
    pn = jnp.where(ok_n, jnp.exp(sn - m_n), 0.0)
    l_n = jnp.sum(pn, axis=1, keepdims=True)
    eb[s, :HE] = jnp.dot(pn.astype(BF), kvn[:, HD:], preferred_element_type=F32).astype(BF)
    tile = place.astype(F32)
    for i, term in enumerate(terms(m_n) + terms(l_n)):
        tile = jnp.where(lane_e == i, term, tile)
    eb[s, HE:] = tile.astype(BF)

    chips = N // 2
    chip = s // 2

    def ecopy(i):
        return remote(eb.at[s], eb.at[s], e_s.at[i], e_r.at[i], (((chip + i) % chips) * 2 + core, t))

    def egive(i):
        src = ((chip + chips - i) % chips) * 2 + core
        return remote(eb.at[src], eb.at[src], eg_s.at[i], eg_r.at[i], mate)

    for i in range(1, chips):
        ecopy(i).start()
    egive(0).start()

    for pc in range(PA):
        ycopy(1 - x, 0, pc).wait_recv()
    for way in (0, 1):
        give(2 + way, section_of(x, (y + 3 - 2 * way) % 4, core))
    for pc in range(PA):
        ycopy(1 - x, 1, pc).wait_recv()
        ylast(1 - x, pc).start()
    for pc in range(PA):
        ycopy(x, 1, pc).wait_recv()
    for way in (0, 1):
        give(4 + way, section_of(1 - x, (y + 3 - 2 * way) % 4, core))
    for way in (x, 1 - x):
        for pc in range(PA):
            ylast(way, pc).wait_recv()
        give(6 + way, section_of(way, (y + 2) % 4, core))
    for i in range(1, chips):
        ecopy(i).wait_recv()
        egive(i).start()
    wo_copy.wait()
    for i in range(8):
        remote(att.at[s], att.at[s], c_s.at[i], c_r.at[i], mate).wait_recv()

    def project(slot_, off):
        zz = (z + off) % 8
        a = jnp.concatenate([att[zz, :, :heads * HD], att[8 + zz, :, :heads * HD]], 0)
        v = jnp.dot(a, wo[...], preferred_element_type=F32)
        pz[slot_, 0] = v[:rows]
        pz[slot_, 1] = v[rows:]

    def off_of(slot_):
        k = (slot_ + 1) // 2
        return jnp.where(slot_ % 2 == 1, 4 - k, 4 + k) % 8

    def cut(r, pc):
        step = rows // PZ[r]
        return pl.ds(pc * step, step)

    def rs(way, k, r, pc):
        part = cut(r, pc)
        return remote(sbuf.at[way, k, r, part], rbuf.at[way, k, r, part],
                      rs_s.at[way, k, r, pc], rs_r.at[way, k, r, pc], zdev(way))

    def rs_send(way, k, r, add):
        for pc in range(PZ[r]):
            part = cut(r, pc)
            v = pz[0 if k == 0 else 2 * k - 1 + way, r, part]
            if add:
                rs(way, k - 1, r, pc).wait_recv()
                v = v + rbuf[way, k - 1, r, part].astype(F32)
            sbuf[way, k, r, part] = v.astype(BF)
            rs(way, k, r, pc).start()

    @pl.loop(0, 8)
    def _(i):
        project(i, off_of(i))

    for i in range(chips):
        egive(i).wait_recv()
    ef[...] = eb[...].astype(F32)
    NE = N * E
    eye = lax.broadcasted_iota(jnp.int32, (NE, NE), 0) == lax.broadcasted_iota(jnp.int32, (NE, NE), 1)
    before = lax.broadcasted_iota(jnp.int32, (NE, NE), 1) < lax.broadcasted_iota(jnp.int32, (NE, NE), 0)

    def across(col):
        return jnp.sum(jnp.where(eye, col, 0.0), axis=0, keepdims=True)

    def three(v, i, step):
        return v[:, i:i + 1] + v[:, i + step:i + step + 1] + v[:, i + 2 * step:i + 2 * step + 1]

    info = ef[:, pl.ds(HE, E), :].reshape(NE, 128)
    id_col = info[:, 6:7] * rows + info[:, 7:8]
    id_row = across(id_col)
    idr[...] = jnp.broadcast_to(id_row, idr.shape)
    same = id_col == id_row
    first = jnp.sum(jnp.where(jnp.logical_and(same, before), 1.0, 0.0), axis=1, keepdims=True) < 0.5
    pick_rows = (id_col == lax.broadcasted_iota(jnp.int32, (NE, N * rows), 1).astype(F32)).astype(F32).astype(BF)
    old = jnp.dot(pick_rows, att[...].reshape(N * rows, -1), preferred_element_type=F32)
    old_stats = old[:, heads * HD:]
    for h in range(heads):
        info = ef[:, pl.ds(HE + h * E, E), :].reshape(NE, 128)
        m_row = across(three(info, 0, 1))
        l_row = across(three(info, 3, 1))
        m_old = three(old_stats, h, heads)
        l_old = three(old_stats, 3 * heads + h, heads)
        logit = jnp.where(same, m_row, NEG_LARGE)
        top = jnp.maximum(m_old, jnp.max(logit, axis=1, keepdims=True))
        w = jnp.where(same, jnp.exp(logit - top), 0.0)
        kept = jnp.exp(m_old - top) * l_old
        total = kept + jnp.sum(w * l_row, axis=1, keepdims=True)
        old_h = old[:, h * HD:(h + 1) * HD]
        new = ef[:, pl.ds(h * E, E), :].reshape(NE, HD).astype(BF)
        joined = (kept * old_h + jnp.dot(w.astype(BF), new, preferred_element_type=F32)) / total
        diff = jnp.where(first, joined - old_h, 0.0)
        hi = diff.astype(BF)
        dh[:, h * HD:(h + 1) * HD] = hi
        dl[:, h * HD:(h + 1) * HD] = (diff - hi.astype(F32)).astype(BF)
    diff = (jnp.dot(dh[...], wo[...], preferred_element_type=F32)
            + jnp.dot(dl[...], wo[...], preferred_element_type=F32))
    dwh[...] = diff.astype(BF)
    dwl[...] = (diff - dwh[...].astype(F32)).astype(BF)

    def correct(slot_, off):
        zz = (z + off) % 8
        at = lax.broadcasted_iota(jnp.int32, (2 * rows, NE), 0)
        at = (at + zz * rows + jnp.where(at >= rows, 7 * rows, 0)).astype(F32)
        put = (at == idr[0:1, :]).astype(F32).astype(BF)
        v = (jnp.dot(put, dwh[...], preferred_element_type=F32)
             + jnp.dot(put, dwl[...], preferred_element_type=F32))
        pz[slot_, 0] = pz[slot_, 0] + v[:rows]
        pz[slot_, 1] = pz[slot_, 1] + v[rows:]

    correct(0, 4)
    for r in (0, 1):
        rs_send(r, 0, r, False)

    @pl.loop(1, 3)
    def _(i):
        correct(i, off_of(i))

    for r in (0, 1):
        rs_send(1 - r, 1, r, False)

    @pl.loop(3, 8)
    def _(i):
        correct(i, off_of(i))

    for k in (1, 2, 3):
        for r in (0, 1):
            rs_send(r, k, r, True)
            if k > 1:
                rs_send(1 - r, k, r, True)

    PR = rows // PP

    def pair_copy(r, pc):
        part = pl.ds(pc * PR, PR)
        return remote(xs.at[r, part], xr.at[r, part], px_s.at[r, pc], px_r.at[r, pc], hpeer)

    for r in (0, 1):
        for pc in range(PZ[r]):
            part = cut(r, pc)
            for way in (0, 1):
                rs(way, 3, r, pc).wait_recv()
            v = pz[7, r, part] + rbuf[0, 3, r, part].astype(F32) + rbuf[1, 3, r, part].astype(F32)
            pz[7, r, part] = v
            xs[r, part] = v.astype(BF)
            if (pc + 1) % (PZ[r] // PP) == 0:
                pair_copy(r, pc // (PZ[r] // PP)).start()

    def blk_of(way, k, r):
        return r * 8 + (z + 8 + (2 * way - 1) * k) % 8

    def ag(way, k, r, pc):
        ref = mgf.at[core, blk_of(way, k, r), cut(r, pc)]
        return remote(ref, ref, ag_s.at[way, k, r, pc], ag_r.at[way, k, r, pc], zdev(way))

    def hand(r, i, blk):
        ref = mgf.at[core, blk]
        remote(ref, ref, mt_s.at[r, i], mt_r.at[r, i], mate).start()

    def hand_wait(r):
        for i in range(8):
            ref = mgf.at[core, t]
            remote(ref, ref, mt_s.at[r, i], mt_r.at[r, i], mate).wait_recv()

    def ag_step(k, r):
        for pc in range(PZ[r]):
            for way in (0, 1):
                ag(way, k - 1, r, pc).wait_recv()
                if k < 3 or way == r:
                    ag(way, k, r, pc).start()
        for way in (0, 1):
            hand(r, 2 * (k - 1) + 1 + way, blk_of(way, k, r))

    def ag_end(r):
        for pc in range(PZ[r]):
            ag(r, 3, r, pc).wait_recv()
        hand(r, 7, blk_of(0, 4, r))

    def ag_begin(r):
        for pp in range(PP):
            part = pl.ds(pp * PR, PR)
            pair_copy(r, pp).wait_recv()
            proj = pz[7, r, part] + xr[r, part].astype(F32)
            mixed = proj + jnp.where(xh == r, res[part].astype(F32), resx[part].astype(F32))
            mgf[core, blk_of(0, 0, r), part] = (mixed * gain[...].reshape(1, -1).astype(F32)).astype(BF)
            for pc in range(pp * PZ[r] // PP, (pp + 1) * PZ[r] // PP):
                for way in (0, 1):
                    ag(way, 0, r, pc).start()

            @pl.when(xh == r)
            def _():
                proj_out[part] = proj
                sq[part] = jnp.sum(mixed * mixed, axis=1, keepdims=True) + jnp.zeros((PR, sq.shape[1]), F32)
        hand(r, 0, blk_of(0, 0, r))

    def sq_copy(i):
        return remote(sq, sqr.at[i], sqs, sqrs.at[i], (t, t))

    def dg_copy(i):
        return remote(fin, fin, dgs.at[i], dgr, (s, (t + i) % N))

    res_copy().wait_recv()
    ag_begin(0)
    ag_step(1, 0)
    ag_begin(1)

    @pl.when(off_diag)
    def _():
        sq_copy((s - t + N) % N).start()

    ag_step(2, 0)
    ag_step(1, 1)
    ag_step(3, 0)
    ag_step(2, 1)
    ag_end(0)

    R = 2 * rows
    FFN = gate.shape[1]
    CB = FFN - CA
    H = CA // 2
    BR = R // PB
    XR = R // PX
    for c in (0, 1):
        @pl.when(core == c)
        def _():
            w_own(c).wait()
            w_far(c).wait_recv()

    def yoff(k):
        return (y + jnp.where(k == 0, 2, jnp.where(k == 1, 1, jnp.where(k == 2, 3, 0)))) % 4

    def ffn_part(hf, pos, hx):
        k = (0, 2 - hx, 1 + hx, 3)[pos]
        b = hx * 8 + 2 * yoff(k)
        a0 = mgf[0, pl.ds(b, 2)].reshape(R, -1)
        a1 = mgf[1, pl.ds(b, 2)].reshape(R, -1)

        def cols(c0, c1):
            return (jnp.dot(a0, wf[0, :, c0:c1], preferred_element_type=F32)
                    + jnp.dot(a1, wf[1, :, c0:c1], preferred_element_type=F32))

        pb[hf, pos] = cols(CA, FFN)
        pa[hf, pos] = cols(0, CA)

        @pl.when(hx != x)
        def _():
            for pc in range(PX):
                part = pl.ds(pc * XR, XR)
                xas[pos, part] = pa[hf, pos, part].astype(BF)
                xacopy(pos, pc).start()

    def bcopy(way, m, pc):
        part = pl.ds(pc * BR, BR)
        return remote(bs.at[way, m, part], br.at[way, m, part], bss.at[way, m, pc], brs.at[way, m, pc], ydev(way))

    def acopy(way, m, pc):
        part = pl.ds(pc * XR, XR)
        return remote(as_.at[way, m, part], ar.at[way, m, part], ass.at[way, m, pc], ars.at[way, m, pc], ydev(way))

    def xacopy(k, pc):
        part = pl.ds(pc * XR, XR)
        return remote(xas.at[k, part], xar.at[k, part], xass.at[k, pc], xars.at[k, pc], xpeer)

    def xbcopy(pc):
        part = pl.ds(pl.multiple_of(pc * BR, BR), BR)
        return remote(xbs.at[part], xbr.at[part], xbss.at[pc], xbrs.at[pc], xpeer)

    def b_send(hf, pos, way, m, pieces=range(PB)):
        for pc in pieces:
            part = pl.ds(pc * BR, BR)
            v = pb[hf, pos, part]
            if m == 2:
                bcopy(way, 0, pc).wait_recv()
                v = v + br[way, 0, part].astype(F32)
            bs[way, m, part] = v.astype(BF)
            bcopy(way, m, pc).start()

    hand_wait(0)
    ffn_part(0, 0, 0)
    b_send(0, 0, 0, 0)
    ag_step(3, 1)
    ffn_part(0, 1, 0)
    b_send(0, 1, 1, 1)
    ag_end(1)
    ffn_part(0, 2, 0)
    ffn_part(0, 3, 0)
    b_send(0, 2, 0, 2, range(PB // 2))
    hand_wait(1)
    ffn_part(1, 0, 1)
    b_send(1, 0, 1, 0)
    b_send(0, 2, 0, 2, range(PB // 2, PB))
    ffn_part(1, 1, 1)
    b_send(1, 1, 0, 1)
    ffn_part(1, 2, 1)
    ffn_part(1, 3, 1)

    ho = x

    def a_sum(pos, pc):
        part = pl.ds(pc * XR, XR)
        xacopy(pos, pc).wait_recv()
        pa[ho, pos, part] = pa[ho, pos, part] + xar[pos, part].astype(F32)

    def a_pos(way):
        return jnp.where(way == x, 2, 1)

    for pc in range(PX):
        part = pl.ds(pc * XR, XR)
        a_sum(0, pc)
        for way in (0, 1):
            as_[way, 0, part] = pa[ho, 0, part, way * H:(way + 1) * H].astype(BF)
            acopy(way, 0, pc).start()
    b_send(1, 2, 1, 2)
    for pc in range(PX):
        part = pl.ds(pc * XR, XR)
        a_sum(1, pc)
        a_sum(2, pc)
        for way in (0, 1):
            as_[way, 1, part] = pa[ho, a_pos(way), part, (1 - way) * H:(2 - way) * H].astype(BF)
            acopy(way, 1, pc).start()
    def order(i):
        return (2 * (1 - core) + i) % PB if PB == 4 else i

    def b_join(hf, hx, pc):
        part = pl.ds(pl.multiple_of(pc * BR, BR), BR)
        bcopy(hx, 2, pc).wait_recv()
        bcopy(1 - hx, 1, pc).wait_recv()
        return pb[hf, 3, part] + br[hx, 2, part].astype(F32) + br[1 - hx, 1, part].astype(F32)

    for pc in range(PX):
        part = pl.ds(pc * XR, XR)
        for way in (0, 1):
            acopy(way, 0, pc).wait_recv()
            as_[way, 2, part] = (pa[ho, a_pos(way), part, way * H:(way + 1) * H]
                                 + ar[way, 0, part].astype(F32)).astype(BF)
            acopy(way, 2, pc).start()

    for i in range(PB):
        pc = order(i)
        part = pl.ds(pl.multiple_of(pc * BR, BR), BR)
        xbs[part] = b_join(1 - ho, 1 - x, pc).astype(BF)
        xbcopy(pc).start()

    @pl.when(diag)
    def _():
        acc_sq = sq[...]
        for i in range(1, N):
            sq_copy(i).wait_recv()
            acc_sq = acc_sq + sqr[i]
        fin[...] = acc_sq
        for i in range(1, N):
            dg_copy(i).start()

    for pc in range(PX):
        part = pl.ds(pc * XR, XR)
        a_sum(3, pc)
        for way in (0, 1):
            acopy(way, 1, pc).wait_recv()
            acopy(way, 2, pc).wait_recv()
        for h in (0, 1):
            pa[ho, 3, part, h * H:(h + 1) * H] = (pa[ho, 3, part, h * H:(h + 1) * H]
                                                  + ar[h, 2, part].astype(F32) + ar[1 - h, 1, part].astype(F32))

    give_rows = pl.multiple_of((1 - core) * rows, rows)
    keep_rows = pl.multiple_of(core * rows, rows)

    def pcopy(i):
        c = (slice(0, CA), slice(CA, FFN))[i]
        return remote(ps.at[:, c], pr.at[:, c], pss.at[i], prs.at[i], mate)

    ps[:, :CA] = pa[ho, 3, pl.ds(give_rows, rows), :]
    pcopy(0).start()
    for i in range(PB):
        pc = order(i)
        part = pl.ds(pl.multiple_of(pc * BR, BR), BR)
        pb[ho, 3, part] = b_join(ho, x, pc)
    for i in range(PB):
        pc = order(i)
        part = pl.ds(pl.multiple_of(pc * BR, BR), BR)
        xbcopy(pc).wait_recv()
        pb[ho, 3, part] = pb[ho, 3, part] + xbr[part].astype(F32)
        if i == PB // 2 - 1:
            ps[:, CA:] = pb[ho, 3, pl.ds(give_rows, rows), :]
            pcopy(1).start()

    @pl.when(off_diag)
    def _():
        dg_copy(1).wait_recv()

    inv = lax.rsqrt(fin[:, :1] / (gate.shape[0] * N) + EPSILON)

    def finish(i, own, c0, c1):
        pcopy(i).wait_recv()
        other = pr[:, c0:c1] * inv
        own = own * inv
        g = jnp.where(core == 0, own, other)
        u = jnp.where(core == 0, other, own)
        hid[:, c0:c1] = g / (1.0 + jnp.exp(-g)) * u

    finish(0, pa[ho, 3, pl.ds(keep_rows, rows), :], 0, CA)
    finish(1, pb[ho, 3, pl.ds(keep_rows, rows), :], CA, FFN)

    @pl.loop(1, N)
    def _(i):
        exchange(tb, tr, t_s, t_r, i).wait_send()
        exchange(qs, qr, q_s, q_r, i).wait_send()

    for i in range(8):
        remote(att.at[s], att.at[s], c_s.at[i], c_r.at[i], mate).wait_send()
        for r in (0, 1):
            ref = mgf.at[core, t]
            remote(ref, ref, mt_s.at[r, i], mt_r.at[r, i], mate).wait_send()
    res_copy().wait_send()
    for i in range(chips):
        egive(i).wait_send()
        if i:
            ecopy(i).wait_send()
    for pc in range(PA):
        xcopy(pc).wait_send()
        for way in (0, 1):
            ycopy(way, 0, pc).wait_send()
            ycopy(way, 1, pc).wait_send()
            ylast(way, pc).wait_send()
    for way in (0, 1):
        for pc in range(PP):
            pair_copy(way, pc).wait_send()
        for r in (0, 1):
            for pc in range(PZ[r]):
                for k in range(4):
                    if k > 0 or way == r:
                        rs(way, k, r, pc).wait_send()
                    if k < 3 or way == r:
                        ag(way, k, r, pc).wait_send()
        for m in range(3):
            for pc in range(PB):
                bcopy(way, m, pc).wait_send()
            for pc in range(PX):
                acopy(way, m, pc).wait_send()
    for pc in range(PB):
        xbcopy(pc).wait_send()
    for k in range(4):
        for pc in range(PX):
            xacopy(k, pc).wait_send()
    for i in (0, 1):
        pcopy(i).wait_send()
    for c in (0, 1):
        @pl.when(core == c)
        def _():
            w_far(c).wait_send()

    @pl.when(diag)
    def _():
        for i in range(1, N):
            dg_copy(i).wait_send()

    @pl.when(off_diag)
    def _():
        sq_copy((s - t + N) % N).wait_send()


def body(
    queries,
    kv_pool,
    block_table,
    cached_lengths,
    arrivals,
    arrival_section,
    arrival_row,
    out_weight,
    residual,
    norm_gain,
    gate_weight,
    up_weight,
):
    rows, heads, hd = queries.shape
    width, ffn = gate_weight.shape
    m = CAP * heads
    entries = arrival_section.shape[0]
    cb = ffn - CA
    vm = pl.BlockSpec(memory_space=pltpu.VMEM)
    hbm = pl.BlockSpec(memory_space=pl.ANY)
    sm = pl.BlockSpec(memory_space=pltpu.SMEM)
    dma = pltpu.SemaphoreType.DMA

    def v(*shape, dtype=BF):
        return pltpu.VMEM(shape, dtype)

    scratch = [
        v(*kv_pool.shape[1:]), v(*arrivals.shape[1:]),
        v(N, m, 128), v(N, m, 128),
        v(N, m, hd), v(N, m, hd),
        v(N, 2 * heads * entries, hd), v(N, 2 * heads * entries, hd, dtype=F32),
        v(rows * heads, hd, dtype=F32),
        v(N, rows, heads * hd + 128), v(*out_weight.shape),
        v(N * entries, heads * hd), v(N * entries, heads * hd),
        v(N * entries, width), v(N * entries, width), v(8, N * entries, dtype=F32),
        v(8, 2, rows, width, dtype=F32), v(2, 4, 2, rows, width), v(2, 4, 2, rows, width),
        v(2, rows, width), v(2, rows, width), v(rows, width), v(2, N, rows, width), v(2, width, ffn),
        v(2, 4, 2 * rows, cb, dtype=F32), v(2, 4, 2 * rows, CA, dtype=F32),
        v(2, 3, 2 * rows, cb), v(2, 3, 2 * rows, cb),
        v(2, 3, 2 * rows, CA // 2), v(2, 3, 2 * rows, CA // 2),
        v(4, 2 * rows, CA), v(4, 2 * rows, CA),
        v(2 * rows, cb), v(2 * rows, cb),
        v(rows, ffn, dtype=F32), v(rows, ffn, dtype=F32),
        v(rows, 128, dtype=F32), v(N, rows, 128, dtype=F32), v(rows, 128, dtype=F32),
        dma((4,)), dma((N,)), dma((N,)), dma((N,)), dma((N,)),
        dma((N // 2,)), dma((N // 2,)), dma((N // 2,)), dma((N // 2,)),
        dma((2, 4, PA)), dma((2, 4, PA)), dma((8,)), dma((8,)),
        dma((2, 4, 2, 4)), dma((2, 4, 2, 4)), dma((2, PP)), dma((2, PP)), dma((2, 4, 2, 4)), dma((2, 4, 2, 4)), dma, dma,
        dma((2, 8)), dma((2, 8)),
        dma, dma, dma((2, 3, PB)), dma((2, 3, PB)), dma((2, 3, PX)), dma((2, 3, PX)),
        dma((4, PX)), dma((4, PX)), dma((PB,)), dma((PB,)), dma((2,)), dma((2,)),
        dma, dma((N,)), dma((N,)), dma,
    ]
    return pl.pallas_call(
        layer_kernel,
        out_shape=(jax.ShapeDtypeStruct(residual.shape, F32), jax.ShapeDtypeStruct((rows, ffn), F32)),
        in_specs=[sm, sm, vm, vm, vm, hbm, hbm, hbm, vm, vm, hbm, hbm],
        out_specs=(vm, vm),
        scratch_shapes=scratch,
        compiler_params=pltpu.CompilerParams(
            collective_id=1, has_side_effects=True, vmem_limit_bytes=VMEM_LIMIT),
        name="layer",
    )(arrival_section, arrival_row, queries.reshape(rows * heads, hd), block_table.T, cached_lengths,
      kv_pool, arrivals, out_weight, residual, norm_gain, gate_weight, up_weight)


def solution(mesh):
    placed = (
        P("section", "tensor", None),
        P(None, "section", None, None),
        P("section", None),
        P("section"),
        P(None, "section", None, None),
        P("section"),
        P("section"),
        P("tensor", "section"),
        P("tensor", "section"),
        P("section"),
        P("section", "tensor"),
        P("section", "tensor"),
    )
    return jax.shard_map(
        body,
        mesh=mesh,
        in_specs=placed,
        out_specs=(P("tensor", "section"), P("section", "tensor")),
        check_vma=False,
    )
```

time: 130 us -> 117 us (0.900)
  Pallas kernels: 124 us -> 112 us
    pallas_call x1, Pallas kernels: 124 us -> 112 us  [body(): pl.pallas_call(layer_kernel, out_shape=(jax.ShapeDtypeStruct(residual.sha...]
where the time goes in v4:
time: 117 us; the launch traced here: 116 us
  Pallas kernels  112 us (96%)
  local copies, waits for them, and re-layouts  3.41 us (3%)
    pallas_call x1, Pallas kernels, body(): pl.pallas_call(layer_kernel, out_shape=(jax.ShapeDtypeStruct(residual.sha...  112 us
    unnamed x2, local copies, waits for them, and re-layouts  3.41 us

profile of v4, /device:TPU:1, one launch (start us, length us, event | category | flops | bytes accessed | tf_op | source)
XLA Modules:
  0.0 115.8 jit_solution(15345644127507247574)
XLA Ops:
  0.6 111.7 %layer.1 = (f32[64,768]{1,0:T(8,128)}, f32[64,1664]{1,0:T(8,128)}) custom-call(s32[8]{0:T(128)} %sec.1, s32[8]{0:T(128)} %row.1, bf16[512,128]{1,0:T(8,128)(2,1)} %bitcast.2, s32[4,64]{1,0:T(4,128)} %bitcast.3, s32[64]{0:T(128)} %lens.1, bf16[8,4,128,256]{3,2,1,0:T(8,128)(2,1)} %pool.1, bf16[8,8,128,256]{3,2,1,0:T(8,128)(2,1)} %arr.1, ...), custom_call_target="tpu_custom_call" | custom-call | tf_op jit(solution)/shard_map/layer/pallas_call | solution.py:788
  112.4 1.6 %copy.16 = f32[64,768]{1,0:T(8,128)} copy(f32[64,768]{1,0:T(8,128)} %get-tuple-element.4) | data formatting | bytes 393216
  114.0 1.8 %copy.17 = f32[64,1664]{1,0:T(8,128)} copy(f32[64,1664]{1,0:T(8,128)} %get-tuple-element.5) | data formatting | bytes 851968

commit v5 on v4

--- a/solution.py
+++ b/solution.py
@@ -13,7 +13,7 @@
 BF = jnp.bfloat16
 F32 = jnp.float32
 N = 16
-CA = 512
+CA = 768
 PZ = (4, 2)
 PP = 2
 PA = 2
@@ -68,10 +68,6 @@
     for dev in (zdev(0), zdev(1), hpeer):
         signal(barrier, dev)
 
-    @pl.when(off_diag)
-    def _():
-        signal(barrier, (s, s))
-
     pool_copy = pltpu.make_async_copy(pool.at[t // 2], kvp, l_sem.at[0])
     arr_copy = pltpu.make_async_copy(arr.at[t // 2], kva, l_sem.at[1])
     wo_copy = pltpu.make_async_copy(wo_in, wo, l_sem.at[2])
@@ -117,13 +113,7 @@
         def _(i):
             exchange(src, dst, ss, rs, i).wait_recv()
 
-    @pl.when(diag)
-    def _():
-        pl.semaphore_wait(barrier, 2 * (N - 1) + 3)
-
-    @pl.when(off_diag)
-    def _():
-        pl.semaphore_wait(barrier, N - 1 + 3)
+    pl.semaphore_wait(barrier, N - 1 + 3)
 
     start_all(tb, tr, t_s, t_r)
     tr[s] = tb[s]
@@ -469,8 +459,37 @@
     def sq_copy(i):
         return remote(sq, sqr.at[i], sqs, sqrs.at[i], (t, t))
 
-    def dg_copy(i):
-        return remote(fin, fin, dgs.at[i], dgr, (s, (t + i) % N))
+    def fin_copy(way):
+        return remote(fin, fin, dgs.at[way], dgr, zdev(way))
+
+    def fin_pair():
+        return remote(fin, fin, dgs.at[2], dgr, hpeer)
+
+    dz = (z + 8 - s % 8) % 8
+    hops = jnp.where(dz <= 4, dz, 8 - dz) + jnp.where(xh == s // 8, 0, 1)
+    on_right = dz <= 3
+    on_left = jnp.logical_or(dz == 0, dz >= 6)
+
+    def spread_step(p):
+        @pl.when(hops == p)
+        def _():
+            if p == 0:
+                total_sq = sq[...]
+                for i in range(1, N):
+                    sq_copy(i).wait_recv()
+                    total_sq = total_sq + sqr[i]
+                fin[...] = total_sq
+                fin_pair().start()
+            else:
+                fin_copy(0).wait_recv()
+
+            @pl.when(on_right)
+            def _():
+                fin_copy(0).start()
+
+            @pl.when(on_left)
+            def _():
+                fin_copy(1).start()
 
     res_copy().wait_recv()
     ag_begin(0)
@@ -486,6 +505,7 @@
     ag_step(3, 0)
     ag_step(2, 1)
     ag_end(0)
+    spread_step(0)
 
     R = 2 * rows
     FFN = gate.shape[1]
@@ -554,18 +574,22 @@
     ag_step(3, 1)
     ffn_part(0, 1, 0)
     b_send(0, 1, 1, 1)
+    spread_step(1)
     ag_end(1)
     ffn_part(0, 2, 0)
     ffn_part(0, 3, 0)
     b_send(0, 2, 0, 2, range(PB // 2))
+    spread_step(2)
     hand_wait(1)
     ffn_part(1, 0, 1)
     b_send(1, 0, 1, 0)
     b_send(0, 2, 0, 2, range(PB // 2, PB))
+    spread_step(3)
     ffn_part(1, 1, 1)
     b_send(1, 1, 0, 1)
     ffn_part(1, 2, 1)
     ffn_part(1, 3, 1)
+    spread_step(4)
 
     ho = x
 
@@ -584,6 +608,7 @@
             as_[way, 0, part] = pa[ho, 0, part, way * H:(way + 1) * H].astype(BF)
             acopy(way, 0, pc).start()
     b_send(1, 2, 1, 2)
+    spread_step(5)
     for pc in range(PX):
         part = pl.ds(pc * XR, XR)
         a_sum(1, pc)
@@ -613,16 +638,6 @@
         part = pl.ds(pl.multiple_of(pc * BR, BR), BR)
         xbs[part] = b_join(1 - ho, 1 - x, pc).astype(BF)
         xbcopy(pc).start()
-
-    @pl.when(diag)
-    def _():
-        acc_sq = sq[...]
-        for i in range(1, N):
-            sq_copy(i).wait_recv()
-            acc_sq = acc_sq + sqr[i]
-        fin[...] = acc_sq
-        for i in range(1, N):
-            dg_copy(i).start()
 
     for pc in range(PX):
         part = pl.ds(pc * XR, XR)
@@ -655,10 +670,6 @@
         if i == PB // 2 - 1:
             ps[:, CA:] = pb[ho, 3, pl.ds(give_rows, rows), :]
             pcopy(1).start()
-
-    @pl.when(off_diag)
-    def _():
-        dg_copy(1).wait_recv()
 
     inv = lax.rsqrt(fin[:, :1] / (gate.shape[0] * N) + EPSILON)
 
@@ -723,8 +734,15 @@
 
     @pl.when(diag)
     def _():
-        for i in range(1, N):
-            dg_copy(i).wait_send()
+        fin_pair().wait_send()
+
+    @pl.when(on_right)
+    def _():
+        fin_copy(0).wait_send()
+
+    @pl.when(on_left)
+    def _():
+        fin_copy(1).wait_send()
 
     @pl.when(off_diag)
     def _():
@@ -783,7 +801,7 @@
         dma((2, 8)), dma((2, 8)),
         dma, dma, dma((2, 3, PB)), dma((2, 3, PB)), dma((2, 3, PX)), dma((2, 3, PX)),
         dma((4, PX)), dma((4, PX)), dma((PB,)), dma((PB,)), dma((2,)), dma((2,)),
-        dma, dma((N,)), dma((N,)), dma,
+        dma, dma((N,)), dma((3,)), dma,
     ]
     return pl.pallas_call(
         layer_kernel,

time: 117 us -> 115 us (0.983)
  Pallas kernels: 112 us -> 110 us
    pallas_call x1, Pallas kernels: 112 us -> 110 us  [body(): pl.pallas_call(layer_kernel, out_shape=(jax.ShapeDtypeStruct(residual.sha...]
where the time goes in v5:
time: 115 us; the launch traced here: 114 us
  Pallas kernels  110 us (96%)
  local copies, waits for them, and re-layouts  3.41 us (3%)
    pallas_call x1, Pallas kernels, body(): pl.pallas_call(layer_kernel, out_shape=(jax.ShapeDtypeStruct(residual.sha...  110 us
    unnamed x2, local copies, waits for them, and re-layouts  3.41 us

profile of v5, /device:TPU:1, one launch (start us, length us, event | category | flops | bytes accessed | tf_op | source)
XLA Modules:
  0.0 114.3 jit_solution(12439692139414355150)
XLA Ops:
  0.6 110.3 %layer.1 = (f32[64,768]{1,0:T(8,128)}, f32[64,1664]{1,0:T(8,128)}) custom-call(s32[8]{0:T(128)} %sec.1, s32[8]{0:T(128)} %row.1, bf16[512,128]{1,0:T(8,128)(2,1)} %bitcast.2, s32[4,64]{1,0:T(4,128)} %bitcast.3, s32[64]{0:T(128)} %lens.1, bf16[8,4,128,256]{3,2,1,0:T(8,128)(2,1)} %pool.1, bf16[8,8,128,256]{3,2,1,0:T(8,128)(2,1)} %arr.1, ...), custom_call_target="tpu_custom_call" | custom-call | tf_op jit(solution)/shard_map/layer/pallas_call | solution.py:806
  110.9 1.6 %copy.16 = f32[64,768]{1,0:T(8,128)} copy(f32[64,768]{1,0:T(8,128)} %get-tuple-element.4) | data formatting | bytes 393216
  112.5 1.8 %copy.17 = f32[64,1664]{1,0:T(8,128)} copy(f32[64,1664]{1,0:T(8,128)} %get-tuple-element.5) | data formatting | bytes 851968

commit v6 on v5

--- a/solution.py
+++ b/solution.py
@@ -18,7 +18,7 @@
 PP = 2
 PA = 2
 PB = 4
-PX = 2
+PX = 4
 
 
 def section_of(x, y, core):

time: 115 us -> 116 us (level)
  no operation moved by 1% of the time
where the time goes in v6:
time: 116 us; the launch traced here: 115 us
  Pallas kernels  111 us (96%)
  local copies, waits for them, and re-layouts  3.41 us (3%)
    pallas_call x1, Pallas kernels, body(): pl.pallas_call(layer_kernel, out_shape=(jax.ShapeDtypeStruct(residual.sha...  111 us
    unnamed x2, local copies, waits for them, and re-layouts  3.41 us

profile of v6, /device:TPU:1, one launch (start us, length us, event | category | flops | bytes accessed | tf_op | source)
XLA Modules:
  0.0 114.7 jit_solution(11721657837881509483)
XLA Ops:
  0.6 110.6 %layer.1 = (f32[64,768]{1,0:T(8,128)}, f32[64,1664]{1,0:T(8,128)}) custom-call(s32[8]{0:T(128)} %sec.1, s32[8]{0:T(128)} %row.1, bf16[512,128]{1,0:T(8,128)(2,1)} %bitcast.2, s32[4,64]{1,0:T(4,128)} %bitcast.3, s32[64]{0:T(128)} %lens.1, bf16[8,4,128,256]{3,2,1,0:T(8,128)(2,1)} %pool.1, bf16[8,8,128,256]{3,2,1,0:T(8,128)(2,1)} %arr.1, ...), custom_call_target="tpu_custom_call" | custom-call | tf_op jit(solution)/shard_map/layer/pallas_call | solution.py:806
  111.3 1.6 %copy.16 = f32[64,768]{1,0:T(8,128)} copy(f32[64,768]{1,0:T(8,128)} %get-tuple-element.4) | data formatting | bytes 393216
  112.9 1.8 %copy.17 = f32[64,1664]{1,0:T(8,128)} copy(f32[64,1664]{1,0:T(8,128)} %get-tuple-element.5) | data formatting | bytes 851968
